TPU v7x, 32 devices: a whole 2x2x4 slice. The times are simulated.
32 devices in a mesh: dp: 4 (over x, core), fsdp: 8 (over z, y).
Axes of the slice: x: 2, y: 2, z: 4, core: 2. Of those that a mesh axis runs over, the one named last changes fastest.
Arguments:
- hidden: bfloat16 [4096, 8192], P(('dp', 'fsdp')), may hold values from -6 to 6
- d_attn: bfloat16 [4096, 1024], P(('dp', 'fsdp')), may hold values from -24 to 24
- w_query: bfloat16 [8192, 1024], P('fsdp'), may hold values from -0.0625 to 0.0625
- w_key: bfloat16 [8192, 128], P('fsdp'), may hold values from -0.0625 to 0.0625
- w_value: bfloat16 [8192, 128], P('fsdp'), may hold values from -0.0625 to 0.0625
- cache_keys: bfloat16 [2048, 128], P('fsdp'), may hold values from -700 to 700
- cache_values: bfloat16 [2048, 128], P('fsdp'), may hold values from -6 to 6
- lengths: int32 [4, 4], P('dp'), may hold values from 1 to 768, 1024 in all within a row
Outputs:
- grad_keys: float32 [2048, 128], P('fsdp')
- grad_values: float32 [2048, 128], P('fsdp')
Inputs may be any that keep to these rules, and one draw needn't show every extreme that they name: `lengths`: each row sums to 1024 and its longest conversation has exactly 768 tokens.
All inputs are finite; a program needn't handle non-finite values.
Results may differ from a plain program's by a relative error of at most 0.0075.
The roundings to bfloat16 on the way count: a program that leaves them out, or rounds other values in their place, can miss the bound.
Values may be sent and summed in bfloat16 or wider, within the bound.
No kernel may reach another device: no remote copies, remote signals or barrier semaphores. Data moves between devices by JAX's collectives and lax.ppermute only.
A program may use at most 128 MiB of HBM per device.

v0:
```python
import jax
import jax.numpy as jnp
from jax import lax
from jax.sharding import PartitionSpec as P


def on_device(hidden, d_attn, w_query, w_key, w_value, cache_keys, cache_values, lengths):
    tokens_here = hidden.shape[0]
    q_width = w_query.shape[1]
    head_dim = w_key.shape[1]
    heads = q_width // head_dim
    scale = head_dim ** (-0.5)
    pieces = (
        lax.all_gather(w_query, "fsdp", axis=0, tiled=True),
        lax.all_gather(w_key, "fsdp", axis=0, tiled=True),
        lax.all_gather(w_value, "fsdp", axis=0, tiled=True),
    )
    query_f, key_f, value_f = tuple(
        (jnp.dot(hidden, piece, preferred_element_type=jnp.float32) for piece in pieces)
    )
    query = query_f.astype(jnp.bfloat16)
    keys_own = key_f.astype(jnp.bfloat16)
    values_own = value_f.astype(jnp.bfloat16)
    cache_k, cache_v = (
        lax.all_gather(cache_keys, "fsdp", axis=0, tiled=True),
        lax.all_gather(cache_values, "fsdp", axis=0, tiled=True),
    )
    group_k, group_v = (
        lax.all_gather(keys_own, "fsdp", axis=0, tiled=True),
        lax.all_gather(values_own, "fsdp", axis=0, tiled=True),
    )
    group_tok = group_k.shape[0]
    ends = jnp.cumsum(lengths[0])
    position = jnp.arange(group_tok, dtype=jnp.int32)
    conv = jnp.sum((position[:, None] >= ends[None, :]).astype(jnp.int32), axis=1)
    own = lax.axis_index("fsdp") * tokens_here + jnp.arange(tokens_here, dtype=jnp.int32)
    own_conv = jnp.sum((own[:, None] >= ends[None, :]).astype(jnp.int32), axis=1)
    q_pos = jnp.repeat(own, heads)
    q_conv = jnp.repeat(own_conv, heads)
    allowed = (q_conv[:, None] == conv[None, :]) & (position[None, :] <= q_pos[:, None])
    rows_q = query.reshape(tokens_here * heads, head_dim)
    rows_d = d_attn.reshape(tokens_here * heads, head_dim)
    dims = (((1,), (1,)), ((), ()))
    s_cache = lax.dot_general(rows_q, cache_k, dims, preferred_element_type=jnp.float32) * scale
    s_group = lax.dot_general(rows_q, group_k, dims, preferred_element_type=jnp.float32) * scale
    top = jnp.maximum(
        jnp.max(s_cache, axis=1), jnp.max(jnp.where(allowed, s_group, -jnp.inf), axis=1)
    )
    e_cache = jnp.exp(s_cache - top[:, None])
    e_group = jnp.where(allowed, jnp.exp(s_group - top[:, None]), jnp.float32(0.0))
    total = jnp.sum(e_cache, axis=1) + jnp.sum(e_group, axis=1)
    p_cache = e_cache / total[:, None]
    probs_cache = p_cache.astype(jnp.bfloat16)
    probs_group = (e_group / total[:, None]).astype(jnp.bfloat16)
    attended = jnp.dot(probs_cache, cache_v, preferred_element_type=jnp.float32) + jnp.dot(
        probs_group, group_v, preferred_element_type=jnp.float32
    )
    delta = jnp.sum(rows_d.astype(jnp.float32) * attended, axis=1)
    d_probs = lax.dot_general(rows_d, cache_v, dims, preferred_element_type=jnp.float32)
    d_score = (p_cache * (d_probs - delta[:, None])).astype(jnp.bfloat16)
    back = (((0,), (0,)), ((), ()))
    grad_v = lax.dot_general(probs_cache, rows_d, back, preferred_element_type=jnp.float32)
    grad_k = lax.dot_general(d_score, rows_q, back, preferred_element_type=jnp.float32) * scale
    across = lax.psum((grad_k, grad_v), "dp")
    summed = (
        lax.psum_scatter(across[0], "fsdp", scatter_dimension=0, tiled=True),
        lax.psum_scatter(across[1], "fsdp", scatter_dimension=0, tiled=True),
    )
    return (summed[0], summed[1])


def solution(mesh):
    placed = (
        P(("dp", "fsdp"), None),
        P(("dp", "fsdp"), None),
        P("fsdp", None),
        P("fsdp", None),
        P("fsdp", None),
        P("fsdp", None),
        P("fsdp", None),
        P("dp", None),
    )
    return jax.shard_map(
        on_device,
        mesh=mesh,
        in_specs=placed,
        out_specs=(P("fsdp", None), P("fsdp", None)),
        check_vma=False,
    )
```

profile of v0, /device:TPU:0, one launch (start us, length us, event | category | flops | bytes accessed | tf_op | source)
XLA Modules:
  0.0 553.8 jit_solution(15082996251590648143)
XLA Ops:
  12.7 36.6 %all_gather.22 = bf16[2048,128]{1,0:T(8,128)(2,1)} all-gather(bf16[256,128]{1,0:T(8,128)(2,1)} %param.13), channel_id=1, replica_groups=mesh['dp'=4,'fsdp'=8] {'fsdp'}, dimensions={0}, use_global_device_ids=true | all-gather | bytes 589824 | tf_op jit(solution)/shard_map/all_gather | solution.py:25
  49.3 31.9 %all_gather.25 = bf16[2048,128]{1,0:T(8,128)(2,1)S(1)} all-gather(bf16[256,128]{1,0:T(8,128)(2,1)S(1)} %copy-done.5), channel_id=1, replica_groups=mesh['dp'=4,'fsdp'=8] {'fsdp'}, dimensions={0}, use_global_device_ids=true | all-gather | bytes 589824 | tf_op jit(solution)/shard_map/all_gather | solution.py:26
  81.3 2.3 convolution_convert_fusion.2
  83.6 33.3 %all_gather.24 = bf16[1024,128]{1,0:T(8,128)(2,1)} all-gather(bf16[128,128]{1,0:T(8,128)(2,1)S(1)} %convolution_convert_fusion.2), channel_id=1, replica_groups=mesh['dp'=4,'fsdp'=8] {'fsdp'}, dimensions={0}, use_global_device_ids=true | all-gather | bytes 294912 | tf_op jit(solution)/shard_map/all_gather | solution.py:29
  116.9 5.3 all-gather.8.cloned.1.call-done
  122.2 2.3 convolution_convert_fusion.1
  124.5 33.8 %all_gather.27 = bf16[1024,128]{1,0:T(8,128)(2,1)} all-gather(bf16[128,128]{1,0:T(8,128)(2,1)S(1)} %convolution_convert_fusion.1), channel_id=1, replica_groups=mesh['dp'=4,'fsdp'=8] {'fsdp'}, dimensions={0}, use_global_device_ids=true | all-gather | bytes 294912 | tf_op jit(solution)/shard_map/all_gather | solution.py:30
  158.2 193.8 %all-gather.4.cloned.1.call-done = bf16[8192,1024]{1,0:T(8,128)(2,1)} async-done(((bf16[1024,1024]{1,0:T(8,128)(2,1)}), bf16[8192,1024]{1,0:T(8,128)(2,1)}) %all-gather.4.cloned.1.call-update) | async-done | bytes 16777232 | tf_op jit(solution)/shard_map/all_gather | solution.py:14
  352.0 8.1 %convolution_convert_fusion = bf16[128,1024]{1,0:T(8,128)(2,1)S(1)} fusion(bf16[128,8192]{1,0:T(8,128)(2,1)S(1)} %copy-done, bf16[8192,1024]{1,0:T(8,128)(2,1)} %all-gather.4.cloned.1.call-done), kind=kOutput, calls=%fused_computation.19 | convolution fusion | flops 2147614720 | bytes 19136512 | tf_op jit(solution)/shard_map/dot_general | solution.py:19
  360.3 2.4 multiply_reduce_fusion
  362.7 1.1 select_reduce_fusion
  363.8 1.9 fusion.3
  365.7 1.9 fusion.1
  367.6 2.4 fusion
  370.1 1.7 fusion.8
  371.8 1.5 copy-done.1
  373.3 1.5 fusion.15
  374.9 6.9 %convolution_multiply_fusion = f32[2048,128]{1,0:T(8,128)} fusion(bf16[1024,128]{1,0:T(8,128)(2,1)S(1)} %reshape.52, f32[1024,2048]{1,0:T(8,128)} %copy-done.1, bf16[1024,128]{1,0:T(8,128)(2,1)S(1)} %reshape.55, bf16[2048,128]{1,0:T(8,128)(2,1)S(1)} %all_gather.25, f32[1024]{0:T(1024)S(1)} %fusion.15), kind=kOutput, calls=%fused_computation.10 | convolution fusion | flops 1080295424 | bytes 10489856 | tf_op jit(solution)/shard_map/dot_general | solution.py:63
  381.8 5.6 %fusion.4 = f32[2048,128]{1,0:T(8,128)} fusion(bf16[1024,128]{1,0:T(8,128)(2,1)S(1)} %reshape.55, f32[1024,2048]{1,0:T(8,128)} %copy-done.1), kind=kOutput, calls=%fused_computation.12 | convolution fusion | flops 538968064 | bytes 9699328 | tf_op jit(solution)/shard_map/dot_general | solution.py:62
  387.5 56.0 %reduce-scatter.3.cloned.1.call-done = f32[256,128]{1,0:T(8,128)} async-done(((f32[2048,128]{1,0:T(8,128)}), f32[256,128]{1,0:T(8,128)}) %reduce-scatter.3.cloned.1.call-update) | async-done | bytes 131088 | tf_op jit(solution)/shard_map/reduce_scatter | solution.py:66
  443.6 66.8 %reduce-scatter.5.cloned.1.call-done = f32[256,128]{1,0:T(8,128)} async-done(((f32[2048,128]{1,0:T(8,128)}), f32[256,128]{1,0:T(8,128)}) %reduce-scatter.5.cloned.1.call-update) | async-done | bytes 131088 | tf_op jit(solution)/shard_map/reduce_scatter | solution.py:67
  510.4 33.4 %all-reduce.3.cloned.1.call-done = (f32[256,128]{1,0:T(8,128)}, f32[256,128]{1,0:T(8,128)}) async-done(((f32[256,128]{1,0:T(8,128)}, f32[256,128]{1,0:T(8,128)}), (f32[256,128]{1,0:T(8,128)}, f32[256,128]{1,0:T(8,128)})) %all-reduce.3.cloned.1.call-update) | async-done | bytes 262160 | tf_op jit(solution)/shard_map/psum | solution.py:64
  543.8 1.6 copy.13
  545.4 1.6 copy.14
  (37 shorter events, 5.8 us)
Async XLA Ops:
  7.2 74.1 %copy-start = (bf16[128,8192]{1,0:T(8,128)(2,1)S(1)}, bf16[128,8192]{1,0:T(8,128)(2,1)}, u32[]{:S(2)}) copy-start(bf16[128,8192]{1,0:T(8,128)(2,1)} %param.8) | copy-start | bytes 6291460
  7.2 42.2 %copy-start.5 = (bf16[256,128]{1,0:T(8,128)(2,1)S(1)}, bf16[256,128]{1,0:T(8,128)(2,1)}, u32[]{:S(2)}) copy-start(bf16[256,128]{1,0:T(8,128)(2,1)} %param.14) | copy-start | bytes 196612
  7.2 74.1 %all-gather.6.cloned.1.call-start = ((), (), s32[]{:S(2)}) async-start(), calls=%async_computation.3 | async-start | bytes 2359296 | tf_op jit(solution)/shard_map/all_gather | solution.py:15
  7.9 114.3 %all-gather.8.cloned.1.call-start = ((), (), s32[]{:S(2)}) async-start(), calls=%async_computation.4 | async-start | bytes 2359296 | tf_op jit(solution)/shard_map/all_gather | solution.py:16
  8.7 343.4 %all-gather.4.cloned.1.call-start = ((), (), s32[]{:S(2)}) async-start(), calls=%async_computation.2 | async-start | bytes 18874368 | tf_op jit(solution)/shard_map/all_gather | solution.py:14
  9.4 434.2 %reduce-scatter.3.cloned.1.call-start = ((), (), s32[]{:S(2)}) async-start(), calls=%async_computation.5 | async-start | bytes 1179648 | tf_op jit(solution)/shard_map/reduce_scatter | solution.py:66
  360.3 2.4 copy-start.4
  367.6 2.5 copy-start.3
  370.1 3.2 copy-start.1
  370.1 3.2 copy-start.2
  381.8 128.6 %reduce-scatter.5.cloned.1.call-start = ((), (), s32[]{:S(2)}) async-start(), calls=%async_computation.6 | async-start | bytes 1179648 | tf_op jit(solution)/shard_map/reduce_scatter | solution.py:67
  387.5 156.3 %all-reduce.3.cloned.1.call-start = ((), (), s32[]{:S(2)}) async-start(), calls=%async_computation.7 | async-start | bytes 524288 | tf_op jit(solution)/shard_map/psum | solution.py:64
Sparse Core Ops, SparseCore 0:
  10.1 59.5 all-gather.5
  71.8 50.3 all-gather.7
  124.3 227.6 all-gather.3
  381.9 61.6 reduce-scatter.2
  447.2 63.1 reduce-scatter.4
  512.7 31.0 all-reduce.2
where the time goes:
time: 554 us
  waiting for transfers between devices  357 us (64%)
  blocking collectives  136 us (25%)
  matrix products  31.9 us (6%)
  between operations  14.3 us (3%)
  other arithmetic  7.26 us (1%)
  local copies, waits for them, and re-layouts  7.08 us (1%)
    all_gather x1, waiting for transfers between devices, on_device(): lax.all_gather(w_query, 'fsdp', axis=0, tiled=True)  194 us
    reduce_scatter x1, waiting for transfers between devices, on_device(): lax.psum_scatter(across[1], 'fsdp', scatter_dimension=0, tiled=True)  66.8 us
    reduce_scatter x1, waiting for transfers between devices, on_device(): lax.psum_scatter(across[0], 'fsdp', scatter_dimension=0, tiled=True)  56 us
    all_gather x1, blocking collectives, on_device(): lax.all_gather(cache_keys, 'fsdp', axis=0, tiled=True)  36.6 us
    all_gather x1, blocking collectives, on_device(): lax.all_gather(values_own, 'fsdp', axis=0, tiled=True)  33.8 us
    psum x1, waiting for transfers between devices, on_device(): across = lax.psum((grad_k, grad_v), 'dp')  33.4 us
    all_gather x1, blocking collectives, on_device(): lax.all_gather(keys_own, 'fsdp', axis=0, tiled=True)  33.3 us
    all_gather x1, blocking collectives, on_device(): lax.all_gather(cache_values, 'fsdp', axis=0, tiled=True)  31.9 us
  transfers between devices with their start and end apart: 6, of which 5 were waited for; matrix products, arithmetic and copies ran while one was open for 2% of the time, Pallas kernels for 0%

commit v1 on v0

v1 whole, which is shorter than its diff:
```python
import functools
import math

import jax
import jax.numpy as jnp
from jax import lax
from jax.experimental import pallas as pl
from jax.experimental.pallas import tpu as pltpu
from jax.sharding import PartitionSpec as P

F32 = jnp.float32
BF16 = jnp.bfloat16
VMEM_LIMIT = 56 * 1024 * 1024


def swap(value, axis, size, bit):
    return lax.ppermute(value, axis, [(i, i ^ bit) for i in range(size)])


def bits_down(size):
    bits = []
    bit = size // 2
    while bit:
        bits.append(bit)
        bit //= 2
    return bits


def doubled(block, axis, size):
    block, order = block[None], [0]
    for bit in bits_down(size):
        block = jnp.concatenate([block, swap(block, axis, size, bit)])
        order = order + [o ^ bit for o in order]
    return block, order


def params():
    return pltpu.CompilerParams(vmem_limit_bytes=VMEM_LIMIT)


def run_copies(copies):
    for copy in copies:
        copy.start()
    for copy in copies:
        copy.wait()


def prepare(where, hidden, w_query, w_key, w_value, n_dp, n_fsdp, q_cut):
    inner = n_fsdp // 2
    tokens = hidden.shape[0]
    rows_w, q_width = w_query.shape
    head_dim = w_key.shape[1]
    share = rows_w // n_dp

    def body(where_ref, hidden_ref, wq_ref, wk_ref, wv_ref, *rest):
        sent, part_a, part_b, sems = rest[: inner - 1], rest[-3], rest[-2], rest[-1]
        me, dp = where_ref[0], where_ref[1]
        rows = pl.ds(pl.multiple_of(dp * share, 16), share)
        pairs = [
            (wk_ref.at[rows], part_a.at[:, pl.ds(0, head_dim)]),
            (wv_ref.at[rows], part_a.at[:, pl.ds(head_dim, head_dim)]),
            (wq_ref.at[rows, pl.ds(0, q_cut)], part_a.at[:, pl.ds(2 * head_dim, q_cut)]),
            (wq_ref.at[rows, pl.ds(q_cut, q_width - q_cut)], part_b),
        ]
        for k in range(1, inner):
            for side, bit in enumerate((0, inner)):
                start = pl.multiple_of((me ^ k ^ bit) * rows_w, 128)
                pairs.append(
                    (hidden_ref.at[:, pl.ds(start, rows_w)], sent[k - 1].at[:, pl.ds(side * rows_w, rows_w)])
                )
        run_copies([pltpu.make_async_copy(a, b, sems.at[i]) for i, (a, b) in enumerate(pairs)])

    moved = 2 * (tokens * 2 * rows_w * 2 * (inner - 1) + share * (q_width + 2 * head_dim) * 2)
    out = pl.pallas_call(
        body,
        in_specs=[pl.BlockSpec(memory_space=pltpu.SMEM)] + [pl.BlockSpec(memory_space=pl.ANY)] * 4,
        out_specs=[pl.BlockSpec(memory_space=pl.ANY)] * (inner + 1),
        out_shape=[jax.ShapeDtypeStruct((tokens, 2 * rows_w), BF16)] * (inner - 1)
        + [
            jax.ShapeDtypeStruct((share, 2 * head_dim + q_cut), BF16),
            jax.ShapeDtypeStruct((share, q_width - q_cut), BF16),
        ],
        scratch_shapes=[pltpu.SemaphoreType.DMA((4 + 2 * (inner - 1),))],
        compiler_params=params(),
        cost_estimate=pl.CostEstimate(flops=0, bytes_accessed=moved, transcendentals=0),
        name="prepare",
    )(where, hidden, w_query, w_key, w_value)
    return out[: inner - 1], out[-2], out[-1]


def multiply(where, hidden, received, near, far, order, n_fsdp):
    inner = n_fsdp // 2
    tokens = hidden.shape[0]
    n_dp, share, cols = far.shape
    rows_w = n_dp * share
    step = math.gcd(cols, 256)
    spans = []
    at = 0
    for _, start, wide in near:
        spans.append((start, at, wide))
        at += wide

    def body(where_ref, hidden_ref, *rest):
        blocks = rest[: inner - 1]
        near_refs = rest[inner - 1 : inner - 1 + len(near)]
        far_ref = rest[inner - 1 + len(near)]
        outs = rest[inner + len(near) : 2 * inner + len(near)]
        x_all, w_all, sems = rest[-3:]
        me, dp = where_ref[0], where_ref[1]
        pairs = []
        for side, bit in enumerate((0, inner)):
            start = pl.multiple_of((me ^ bit) * rows_w, 128)
            pairs.append(
                (
                    hidden_ref.at[:, pl.ds(start, rows_w)],
                    x_all.at[pl.ds(0, tokens), pl.ds(side * rows_w, rows_w)],
                )
            )
        for k in range(1, inner):
            pairs.append((blocks[k - 1], x_all.at[pl.ds(k * tokens, tokens)]))
        for ref, (start, to, wide) in zip(near_refs, spans):
            pairs.append((ref.at[:, pl.ds(start, wide)], w_all.at[pl.ds(0, rows_w), pl.ds(to, wide)]))
        for slot, o in enumerate(order):
            to = pl.multiple_of(rows_w + (dp ^ o) * share, 16)
            pairs.append((far_ref.at[slot], w_all.at[pl.ds(to, share)]))
        run_copies([pltpu.make_async_copy(a, b, sems.at[i]) for i, (a, b) in enumerate(pairs)])

        @pl.loop(0, cols // step)
        def _(n):
            at = pl.multiple_of(n * step, 128)
            product = jnp.dot(x_all[...], w_all[:, pl.ds(at, step)], preferred_element_type=F32)
            for k in range(inner):
                outs[k][:, pl.ds(at, step)] = product[k * tokens : (k + 1) * tokens]

    copies = 2 + (inner - 1) + len(near) + n_dp
    moved = inner * tokens * 2 * rows_w * 2 + 2 * rows_w * cols * 2 + inner * tokens * cols * 4
    return pl.pallas_call(
        body,
        in_specs=[pl.BlockSpec(memory_space=pltpu.SMEM)]
        + [pl.BlockSpec(memory_space=pl.ANY)] * (inner + len(near) + 1),
        out_specs=[pl.BlockSpec(memory_space=pltpu.VMEM)] * inner,
        out_shape=[jax.ShapeDtypeStruct((tokens, cols), F32)] * inner,
        scratch_shapes=[
            pltpu.VMEM((inner * tokens, 2 * rows_w), BF16),
            pltpu.VMEM((2 * rows_w, cols), BF16),
            pltpu.SemaphoreType.DMA((copies,)),
        ],
        compiler_params=params(),
        cost_estimate=pl.CostEstimate(
            flops=2 * inner * tokens * 2 * rows_w * cols, bytes_accessed=moved, transcendentals=0
        ),
        name="multiply",
    )(where, hidden, *received, *[ref for ref, _, _ in near], far)


def attend(where, lengths, parts, q_at, d_attn, first_head, n_heads, cache, group, f_order, sums):
    tokens = d_attn.shape[0]
    n_blocks, block, twice = cache.shape
    head_dim = twice // 2
    n_convs = lengths.shape[1]
    scale = head_dim ** (-0.5)
    to_log2 = scale * math.log2(math.e)
    pair = 2 if n_heads % 2 == 0 else 1
    lanes = pair * tokens
    n_cache = n_blocks * block
    n_group = n_blocks * tokens
    chunk = 512
    n_sum = len(sums)
    n_part = len(parts)

    def body(where_ref, len_ref, d_ref, cache_ref, group_ref, *rest):
        part_refs = rest[:n_part]
        sum_refs = rest[n_part : n_part + n_sum]
        keep_ref, give_ref, gk, gv, s_ref, p_ref, q_ref = rest[n_part + n_sum :]
        me, dp = where_ref[0], where_ref[1]

        q_all = part_refs[0][:, pl.ds(q_at, n_heads * head_dim)]
        for ref in part_refs[1:]:
            q_all = q_all + ref[:, pl.ds(q_at, n_heads * head_dim)]
        q_all = q_all.astype(BF16)
        for h in range(n_heads):
            q_ref[h, 0] = q_all[:, h * head_dim : (h + 1) * head_dim]
            at = (first_head + h) * head_dim
            q_ref[h, 1] = d_ref[:, at : at + head_dim]

        q_pos = me * tokens + lax.broadcasted_iota(jnp.int32, (1, lanes), 1) % tokens
        begin = jnp.zeros((1, lanes), jnp.int32)
        end = jnp.int32(0)
        for i in range(n_convs):
            end = end + len_ref[0, i]
            begin = jnp.where(end <= q_pos, end, begin)

        @pl.loop(0, n_heads // pair)
        def _(step):
            rows_q = jnp.concatenate([q_ref[step * pair + i, 0] for i in range(pair)], axis=0)
            rows_d = jnp.concatenate([q_ref[step * pair + i, 1] for i in range(pair)], axis=0)
            dims = (((1,), (1,)), ((), ()))
            top = jnp.full((1, lanes), -jnp.inf, F32)
            cache_spans = [
                (b, r, min(chunk, block)) for b in range(n_blocks) for r in range(0, block, min(chunk, block))
            ]
            for b, r, size in cache_spans:
                s = lax.dot_general(
                    cache_ref[b, r : r + size, :head_dim], rows_q, dims, preferred_element_type=F32
                )
                s_ref[pl.ds(b * block + r, size)] = s
                top = jnp.maximum(top, jnp.max(s, axis=0, keepdims=True))
            for b in range(n_blocks):
                s = lax.dot_general(group_ref[b, :, :head_dim], rows_q, dims, preferred_element_type=F32)
                pos = (me ^ f_order[b]) * tokens + lax.broadcasted_iota(jnp.int32, (tokens, lanes), 0)
                s = jnp.where((pos <= q_pos) & (pos >= begin), s, -jnp.inf)
                s_ref[pl.ds(n_cache + b * tokens, tokens)] = s
                top = jnp.maximum(top, jnp.max(s, axis=0, keepdims=True))
            total = jnp.zeros((1, lanes), F32)
            for r in range(0, n_cache + n_group, chunk):
                e = jnp.exp2((s_ref[pl.ds(r, chunk)] - top) * to_log2)
                s_ref[pl.ds(r, chunk)] = e
                total = total + jnp.sum(e, axis=0, keepdims=True)
            inv = 1.0 / total
            delta = jnp.zeros((1, lanes), F32)
            for b in range(n_blocks):
                p = s_ref[pl.ds(n_cache + b * tokens, tokens)] * inv
                dp_ = lax.dot_general(group_ref[b, :, head_dim:], rows_d, dims, preferred_element_type=F32)
                delta = delta + jnp.sum(p.astype(BF16).astype(F32) * dp_, axis=0, keepdims=True)
            first = n_sum == 0
            for b, r, size in cache_spans:
                at = pl.ds(b * block + r, size)
                p = s_ref[at] * inv
                pb = p.astype(BF16)
                dp_ = lax.dot_general(
                    cache_ref[b, r : r + size, head_dim:], rows_d, dims, preferred_element_type=F32
                )
                s_ref[at] = p
                p_ref[at] = dp_
                delta = delta + jnp.sum(pb.astype(F32) * dp_, axis=0, keepdims=True)
                g = jnp.dot(pb, rows_d, preferred_element_type=F32)
                before = gv[at] if first else gv[at]
                gv[at] = jnp.where(step == 0, 0.0, before) + g
            for b, r, size in cache_spans:
                at = pl.ds(b * block + r, size)
                ds = (s_ref[at] * (p_ref[at] - delta)).astype(BF16)
                g = jnp.dot(ds, rows_q, preferred_element_type=F32)
                gk[at] = jnp.where(step == 0, 0.0, gk[at]) + g

        even = dp % 2 == 0
        if n_sum:
            keep_in, give_in = sum_refs[0][...], sum_refs[1][...]
        else:
            keep_in = give_in = 0.0

        @pl.when(even)
        def _():
            keep_ref[...] = keep_in + gk[...] * scale
            give_ref[...] = give_in + gv[...]

        @pl.when(jnp.logical_not(even))
        def _():
            keep_ref[...] = keep_in + gv[...]
            give_ref[...] = give_in + gk[...] * scale

    rows = n_heads * tokens
    flops = 2 * rows * head_dim * (5 * n_cache + 2 * n_group)
    return pl.pallas_call(
        body,
        in_specs=[pl.BlockSpec(memory_space=pltpu.SMEM)] * 2
        + [pl.BlockSpec(memory_space=pltpu.VMEM)] * (3 + n_part + n_sum),
        out_specs=[pl.BlockSpec(memory_space=pltpu.VMEM)] * 2,
        out_shape=[jax.ShapeDtypeStruct((n_cache, head_dim), F32)] * 2,
        scratch_shapes=[
            pltpu.VMEM((n_cache, head_dim), F32),
            pltpu.VMEM((n_cache, head_dim), F32),
            pltpu.VMEM((n_cache + n_group, lanes), F32),
            pltpu.VMEM((n_cache, lanes), F32),
            pltpu.VMEM((n_heads, 2, tokens, head_dim), BF16),
        ],
        compiler_params=params(),
        cost_estimate=pl.CostEstimate(
            flops=flops,
            bytes_accessed=12 * n_cache * head_dim,
            transcendentals=rows * (n_cache + n_group),
        ),
        name="attend",
    )(where, lengths, d_attn, cache, group, *parts, *sums)


def make_on_device(n_dp, n_fsdp):
    inner = n_fsdp // 2

    def on_device(hidden, d_attn, w_query, w_key, w_value, cache_keys, cache_values, lengths):
        head_dim = w_key.shape[1]
        q_width = w_query.shape[1]
        heads = q_width // head_dim
        me = lax.axis_index("fsdp")
        dp = lax.axis_index("dp")
        where = jnp.stack([me, dp]).astype(jnp.int32)
        heads_a = heads // 4
        q_cut = heads_a * head_dim

        sent, part_a, part_b = prepare(
            where, hidden, w_query, w_key, w_value, n_dp, n_fsdp, q_cut
        )
        part_a = swap(part_a, "fsdp", n_fsdp, inner)
        received = [swap(block, "fsdp", n_fsdp, k + 1) for k, block in enumerate(sent)]
        part_b = swap(part_b, "fsdp", n_fsdp, inner)
        cache, f_order = doubled(
            jnp.concatenate([cache_keys, cache_values], axis=1), "fsdp", n_fsdp
        )
        part_a, *received = lax.optimization_barrier((part_a, *received))
        far_a, d_order = doubled(part_a, "dp", n_dp)
        far_b, _ = doubled(part_b, "dp", n_dp)

        near_a = [(w_key, 0, head_dim), (w_value, 0, head_dim), (w_query, 0, q_cut)]
        near_b = [(w_query, q_cut, q_width - q_cut)]
        own_a, *away_a = multiply(where, hidden, received, near_a, far_a, d_order, n_fsdp)
        own_b, *away_b = multiply(where, hidden, received, near_b, far_b, d_order, n_fsdp)
        parts_a = [own_a] + [swap(x, "fsdp", n_fsdp, k + 1) for k, x in enumerate(away_a)]
        parts_b = [own_b] + [swap(x, "fsdp", n_fsdp, k + 1) for k, x in enumerate(away_b)]
        kv_own = functools.reduce(lambda a, b: a + b, [x[:, : 2 * head_dim] for x in parts_a])
        group, _ = doubled(kv_own.astype(BF16), "fsdp", n_fsdp)

        sums = attend(
            where, lengths, parts_a, 2 * head_dim, d_attn, 0, heads_a, cache, group, f_order, ()
        )
        keep, give = attend(
            where, lengths, parts_b, 0, d_attn, heads_a, heads - heads_a, cache, group, f_order, sums
        )

        half = keep + swap(give, "dp", n_dp, 1)
        size = half.shape[0] // n_fsdp
        mine = half[:size]
        for slot in range(1, n_fsdp):
            out = half[slot * size : (slot + 1) * size].astype(BF16)
            mine = mine + swap(out, "fsdp", n_fsdp, f_order[slot]).astype(F32)
        for bit in bits_down(n_dp)[:-1]:
            mine = mine + swap(mine, "dp", n_dp, bit)
        other = swap(mine, "dp", n_dp, 1)
        even = dp % 2 == 0
        return jnp.where(even, mine, other), jnp.where(even, other, mine)

    return on_device


def solution(mesh):
    placed = (
        P(("dp", "fsdp"), None),
        P(("dp", "fsdp"), None),
        P("fsdp", None),
        P("fsdp", None),
        P("fsdp", None),
        P("fsdp", None),
        P("fsdp", None),
        P("dp", None),
    )
    return jax.shard_map(
        make_on_device(mesh.shape["dp"], mesh.shape["fsdp"]),
        mesh=mesh,
        in_specs=placed,
        out_specs=(P("fsdp", None), P("fsdp", None)),
        check_vma=False,
    )
```

time: 554 us -> 233 us (0.42)
  waiting for transfers between devices: 357 us -> 84 us
  blocking collectives: 136 us -> 0 us
  Pallas kernels: 0 us -> 98.9 us
  starting transfers between devices: 0.24 us -> 39.3 us
  matrix products: 31.9 us -> 0 us
  between operations: 14.3 us -> 0.83 us
  local copies, waits for them, and re-layouts: 7.08 us -> 1.07 us
    all_gather x3 -> x0, waiting for transfers between devices: 199 us -> none  [the longest x1 194 us: on_device(): lax.all_gather(w_query, 'fsdp', axis=0, tiled=True)]
    all_gather x4 -> x0, blocking collectives: 136 us -> none  [the longest x1 36.6 us: on_device(): lax.all_gather(cache_keys, 'fsdp', axis=0, tiled=True)]
    reduce_scatter x2 -> x0, waiting for transfers between devices: 123 us -> none  [the longest x1 66.8 us: on_device(): lax.psum_scatter(across[1], 'fsdp', scatter_dimension=0, tiled=True)]
    pallas_call x0 -> x5, Pallas kernels: none -> 98.9 us  [the longest x1 69.5 us: prepare(): pl.pallas_call(body, in_specs=[pl.BlockSpec(memory_space=pltpu.SMEM)] + [...]
    ppermute x0 -> x31, waiting for transfers between devices: none -> 84 us  [swap(): return lax.ppermute(value, axis, [(i, i ^ bit) for i in range(size)])]
    ppermute x0 -> x31, starting transfers between devices: none -> 39.3 us  [swap(): return lax.ppermute(value, axis, [(i, i ^ bit) for i in range(size)])]
    psum x1 -> x0, waiting for transfers between devices: 33.4 us -> none  [on_device(): across = lax.psum((grad_k, grad_v), 'dp')]
    dot_general x9 -> x0, matrix products: 31.9 us -> none  [the longest x3 12.7 us: on_device(): jnp.dot(hidden, piece, preferred_element_type=jnp.float32)]
  transfers between devices with their start and end apart: 6 -> 31, of which waited for: 5 -> 17; matrix products, arithmetic and copies ran while one was open for 2% -> 2% of each run, Pallas kernels for 0% -> 8%
where the time goes in v1:
time: 233 us
  Pallas kernels  98.9 us (42%)
  waiting for transfers between devices  84 us (36%)
  starting transfers between devices  39.3 us (17%)
  other arithmetic  8.53 us (4%)
    ppermute x31, waiting for transfers between devices, swap(): return lax.ppermute(value, axis, [(i, i ^ bit) for i in range(size)])  84 us
    pallas_call x1, Pallas kernels, prepare(): pl.pallas_call(body, in_specs=[pl.BlockSpec(memory_space=pltpu.SMEM)] + [...  69.5 us
    ppermute x31, starting transfers between devices, swap(): return lax.ppermute(value, axis, [(i, i ^ bit) for i in range(size)])  39.3 us
    pallas_call x2, Pallas kernels, attend(): pl.pallas_call(body, in_specs=[pl.BlockSpec(memory_space=pltpu.SMEM)] * 2...  17.7 us
    pallas_call x2, Pallas kernels, multiply(): pl.pallas_call(body, in_specs=[pl.BlockSpec(memory_space=pltpu.SMEM)] + [...  11.7 us
  transfers between devices with their start and end apart: 31, of which 17 were waited for; matrix products, arithmetic and copies ran while one was open for 2% of the time, Pallas kernels for 8%

profile of v1, /device:TPU:0, one launch (start us, length us, event | category | flops | bytes accessed | tf_op | source)
XLA Modules:
  0.0 232.7 jit_solution(6946330063441340673)
XLA Ops:
  1.3 69.5 %prepare.1 = (bf16[128,2048]{1,0:T(8,128)(2,1)}, bf16[128,2048]{1,0:T(8,128)(2,1)}, bf16[128,2048]{1,0:T(8,128)(2,1)}, bf16[256,512]{1,0:T(8,128)(2,1)}, bf16[256,768]{1,0:T(8,128)(2,1)}) custom-call(s32[2]{0:T(128)} %pad_add_fusion.where_ref, bf16[128,8192]{1,0:T(8,128)(2,1)} %hidden_ref.5, bf16[1024,1024]{1,0:T(8,128)(2,1)} %rest_3_.3, ...), custom_call_target="tpu_custom_call" | custom-call | bytes 4456448 | tf_op jit(solution)/shard_map/prepare/pallas_call | solution.py:74
  70.8 3.0 %collective-permute-start.4 = (bf16[128,2048]{1,0:T(8,128)(2,1)}, bf16[128,2048]{1,0:T(8,128)(2,1)S(1)}, u32[]{:S(2)}, u32[]{:S(2)}) collective-permute-start(bf16[128,2048]{1,0:T(8,128)(2,1)} %get-tuple-element.24), channel_id=1, source_target_pairs={{0,1},{1,0},{2,3},{3,2},{4,5},{5,4},{6,7},{7,6},{8,9},{9,8},{10,11... | collective-permute-start | bytes 1572872 | tf_op jit(solution)/shard_map/ppermute | solution.py:17
  75.4 3.0 %collective-permute-start.3 = (bf16[256,512]{1,0:T(8,128)(2,1)}, bf16[256,512]{1,0:T(8,128)(2,1)S(1)}, u32[]{:S(2)}, u32[]{:S(2)}) collective-permute-start(bf16[256,512]{1,0:T(8,128)(2,1)} %get-tuple-element.23), channel_id=1, source_target_pairs={{0,4},{1,5},{2,6},{3,7},{4,0},{5,1},{6,2},{7,3},{8,12},{9,13},{10,... | collective-permute-start | bytes 786440 | tf_op jit(solution)/shard_map/ppermute | solution.py:17
  78.4 26.5 %collective-permute-done.3 = bf16[256,512]{1,0:T(8,128)(2,1)S(1)} collective-permute-done((bf16[256,512]{1,0:T(8,128)(2,1)}, bf16[256,512]{1,0:T(8,128)(2,1)S(1)}, u32[]{:S(2)}, u32[]{:S(2)}) %collective-permute-start.3) | collective-permute-done | bytes 262176 | tf_op jit(solution)/shard_map/ppermute | solution.py:17
  104.9 7.5 %collective-permute-done.6.rest_2_ = bf16[128,2048]{1,0:T(8,128)(2,1)S(1)} collective-permute-done((bf16[128,2048]{1,0:T(8,128)(2,1)}, bf16[128,2048]{1,0:T(8,128)(2,1)S(1)}, u32[]{:S(2)}, u32[]{:S(2)}) %collective-permute-start.6) | collective-permute-done | bytes 524320 | tf_op jit(solution)/shard_map/ppermute | solution.py:17
  114.5 7.2 %collective-permute-done.7 = bf16[1,256,512]{2,1,0:T(8,128)(2,1)S(1)} collective-permute-done((bf16[1,256,512]{2,1,0:T(8,128)(2,1)S(1)}, bf16[1,256,512]{2,1,0:T(8,128)(2,1)S(1)}, u32[]{:S(2)}, u32[]{:S(2)}) %collective-permute-start.7) | collective-permute-done | bytes 262176 | tf_op jit(solution)/shard_map/ppermute | solution.py:17
  121.9 2.1 collective-permute-start
  124.0 4.1 %collective-permute-done.16 = bf16[1,256,768]{2,1,0:T(8,128)(2,1)S(1)} collective-permute-done((bf16[1,256,768]{2,1,0:T(8,128)(2,1)S(1)}, bf16[1,256,768]{2,1,0:T(8,128)(2,1)S(1)}, u32[]{:S(2)}, u32[]{:S(2)}) %collective-permute-start.16) | collective-permute-done | bytes 393248 | tf_op jit(solution)/shard_map/ppermute | solution.py:17
  129.4 5.3 %multiply.2 = (f32[128,512]{1,0:T(8,128)}, f32[128,512]{1,0:T(8,128)}, f32[128,512]{1,0:T(8,128)}, f32[128,512]{1,0:T(8,128)}) custom-call(s32[2]{0:T(128)} %pad_add_fusion.where_ref, bf16[128,8192]{1,0:T(8,128)(2,1)} %hidden_ref.5, bf16[128,2048]{1,0:T(8,128)(2,1)} %copy-done, bf16[128,2048]{1,0:T(8,128)(2,1)} %copy-done.1, bf16[128,2048]{1,0:T(8,128)(2,1)} %copy-done.2, ...), custom_call_target="tpu_custom_call" | custom-call | flops 1073741824 | bytes 5242880 | tf_op jit(solution)/shard_map/multiply/pallas_call | solution.py:137
  136.1 2.1 collective-permute-start.11
  138.3 5.3 %collective-permute-done.9.rest_1_ = f32[128,512]{1,0:T(8,128)S(1)} collective-permute-done((f32[128,512]{1,0:T(8,128)}, f32[128,512]{1,0:T(8,128)S(1)}, u32[]{:S(2)}, u32[]{:S(2)}) %collective-permute-start.9) | collective-permute-done | bytes 262176 | tf_op jit(solution)/shard_map/ppermute | solution.py:17
  145.4 5.7 %collective-permute-done.11.rest_3_ = f32[128,512]{1,0:T(8,128)S(1)} collective-permute-done((f32[128,512]{1,0:T(8,128)}, f32[128,512]{1,0:T(8,128)S(1)}, u32[]{:S(2)}, u32[]{:S(2)}) %collective-permute-start.11) | collective-permute-done | bytes 262176 | tf_op jit(solution)/shard_map/ppermute | solution.py:17
  154.2 2.4 %collective-permute-done.1 = bf16[2,256,256]{2,1,0:T(8,128)(2,1)S(1)} collective-permute-done((bf16[2,256,256]{2,1,0:T(8,128)(2,1)S(1)}, bf16[2,256,256]{2,1,0:T(8,128)(2,1)S(1)}, u32[]{:S(2)}, u32[]{:S(2)}) %collective-permute-start.1) | collective-permute-done | bytes 262176 | tf_op jit(solution)/shard_map/ppermute | solution.py:17
  157.4 2.4 %collective-permute-start.13 = (bf16[2,128,256]{2,1,0:T(8,128)(2,1)S(1)}, bf16[2,128,256]{2,1,0:T(8,128)(2,1)S(1)}, u32[]{:S(2)}, u32[]{:S(2)}) collective-permute-start(bf16[2,128,256]{2,1,0:T(8,128)(2,1)S(1)} %pad_maximum_fusion.9), channel_id=1, source_target_pairs={{0,2},{1,3},{2,0},{3,1},{4,6},{5,7},{6,4},{7,5},{8,10},{9,11},{10,... | collective-permute-start | bytes 393224 | tf_op jit(solution)/shard_map/ppermute | solution.py:17
  165.2 6.5 %multiply.3 = (f32[128,768]{1,0:T(8,128)}, f32[128,768]{1,0:T(8,128)}, f32[128,768]{1,0:T(8,128)}, f32[128,768]{1,0:T(8,128)}) custom-call(s32[2]{0:T(128)} %pad_add_fusion.where_ref, bf16[128,8192]{1,0:T(8,128)(2,1)} %hidden_ref.5, bf16[128,2048]{1,0:T(8,128)(2,1)} %copy-done, bf16[128,2048]{1,0:T(8,128)(2,1)} %copy-done.1, bf16[128,2048]{1,0:T(8,128)(2,1)} %copy-done.2, ...), custom_call_target="tpu_custom_call" | custom-call | flops 1610612736 | bytes 6815744 | tf_op jit(solution)/shard_map/multiply/pallas_call | solution.py:137
  178.1 5.8 %attend.2 = (f32[2048,128]{1,0:T(8,128)}, f32[2048,128]{1,0:T(8,128)}) custom-call(s32[2]{0:T(128)} %pad_add_fusion.where_ref, s32[1,4]{1,0:T(1,128)} %len_ref.3, bf16[128,1024]{1,0:T(8,128)(2,1)} %d_ref.3, bf16[8,256,256]{2,1,0:T(8,128)(2,1)} %pad_maximum_fusion.1.cache_ref, bf16[8,128,256]{2,1,0:T(8,128)(2,1)} %pad_maximum_fusion.6.group_ref, ...), custom_call_target="tpu_custom_call" | custom-call | flops 805306368 | bytes 3145728 | tf_op jit(solution)/shard_map/attend/pallas_call | solution.py:263
  183.8 8.6 %collective-permute-done.18.rest_1_ = f32[128,768]{1,0:T(8,128)S(1)} collective-permute-done((f32[128,768]{1,0:T(8,128)}, f32[128,768]{1,0:T(8,128)S(1)}, u32[]{:S(2)}, u32[]{:S(2)}) %collective-permute-start.18) | collective-permute-done | bytes 393248 | tf_op jit(solution)/shard_map/ppermute | solution.py:17
  193.5 12.0 %attend.3 = (f32[2048,128]{1,0:T(8,128)}, f32[2048,128]{1,0:T(8,128)}) custom-call(s32[2]{0:T(128)} %pad_add_fusion.where_ref, s32[1,4]{1,0:T(1,128)} %len_ref.3, bf16[128,1024]{1,0:T(8,128)(2,1)} %d_ref.3, bf16[8,256,256]{2,1,0:T(8,128)(2,1)} %pad_maximum_fusion.1.cache_ref, bf16[8,128,256]{2,1,0:T(8,128)(2,1)} %pad_maximum_fusion.6.group_ref, ...), custom_call_target="tpu_custom_call" | custom-call | flops 2415919104 | bytes 3145728 | tf_op jit(solution)/shard_map/attend/pallas_call | solution.py:263
  205.4 2.9 %collective-permute-done.21 = f32[2048,128]{1,0:T(8,128)S(1)} collective-permute-done((f32[2048,128]{1,0:T(8,128)}, f32[2048,128]{1,0:T(8,128)S(1)}, u32[]{:S(2)}, u32[]{:S(2)}) %collective-permute-start.21) | collective-permute-done | bytes 1048608 | tf_op jit(solution)/shard_map/ppermute | solution.py:17
  209.7 2.1 collective-permute-start.22
  214.1 2.9 %collective-permute-start.26 = (bf16[256,128]{1,0:T(8,128)(2,1)S(1)}, bf16[256,128]{1,0:T(8,128)(2,1)S(1)}, u32[]{:S(2)}, u32[]{:S(2)}) collective-permute-start(bf16[256,128]{1,0:T(8,128)(2,1)S(1)} %get-tuple-element.49), channel_id=1, source_target_pairs={{0,5},{1,4},{2,7},{3,6},{4,1},{5,0},{6,3},{7,2},{8,13},{9,12},{10,... | collective-permute-start | bytes 196616 | tf_op jit(solution)/shard_map/ppermute | solution.py:17
  218.5 2.1 collective-permute-start.24
  221.3 2.2 collective-permute-done.26
  227.0 3.5 %collective-permute-done.29 = f32[256,128]{1,0:T(8,128)S(1)} collective-permute-done((f32[256,128]{1,0:T(8,128)S(1)}, f32[256,128]{1,0:T(8,128)S(1)}, u32[]{:S(2)}, u32[]{:S(2)}) %collective-permute-start.29) | collective-permute-done | bytes 131104 | tf_op jit(solution)/shard_map/ppermute | solution.py:17
  (83 shorter events, 37.2 us)
Async XLA Ops:
  70.8 34.1 %collective-permute-start.4 = (bf16[128,2048]{1,0:T(8,128)(2,1)}, bf16[128,2048]{1,0:T(8,128)(2,1)S(1)}, u32[]{:S(2)}, u32[]{:S(2)}) collective-permute-start(bf16[128,2048]{1,0:T(8,128)(2,1)} %get-tuple-element.24), channel_id=1, source_target_pairs={{0,1},{1,0},{2,3},{3,2},{4,5},{5,4},{6,7},{7,6},{8,9},{9,8},{10,11... | collective-permute-start | bytes 1572872 | tf_op jit(solution)/shard_map/ppermute | solution.py:17
  73.8 31.1 %collective-permute-start.5 = (bf16[128,2048]{1,0:T(8,128)(2,1)}, bf16[128,2048]{1,0:T(8,128)(2,1)S(1)}, u32[]{:S(2)}, u32[]{:S(2)}) collective-permute-start(bf16[128,2048]{1,0:T(8,128)(2,1)} %get-tuple-element.25), channel_id=1, source_target_pairs={{0,2},{1,3},{2,0},{3,1},{4,6},{5,7},{6,4},{7,5},{8,10},{9,11},{10,... | collective-permute-start | bytes 1572872 | tf_op jit(solution)/shard_map/ppermute | solution.py:17
  75.4 37.1 %collective-permute-start.6 = (bf16[128,2048]{1,0:T(8,128)(2,1)}, bf16[128,2048]{1,0:T(8,128)(2,1)S(1)}, u32[]{:S(2)}, u32[]{:S(2)}) collective-permute-start(bf16[128,2048]{1,0:T(8,128)(2,1)} %get-tuple-element.26), channel_id=1, source_target_pairs={{0,3},{1,2},{2,1},{3,0},{4,7},{5,6},{6,5},{7,4},{8,11},{9,10},{10,... | collective-permute-start | bytes 1572872 | tf_op jit(solution)/shard_map/ppermute | solution.py:17
  75.4 29.5 %collective-permute-start.3 = (bf16[256,512]{1,0:T(8,128)(2,1)}, bf16[256,512]{1,0:T(8,128)(2,1)S(1)}, u32[]{:S(2)}, u32[]{:S(2)}) collective-permute-start(bf16[256,512]{1,0:T(8,128)(2,1)} %get-tuple-element.23), channel_id=1, source_target_pairs={{0,4},{1,5},{2,6},{3,7},{4,0},{5,1},{6,2},{7,3},{8,12},{9,13},{10,... | collective-permute-start | bytes 786440 | tf_op jit(solution)/shard_map/ppermute | solution.py:17
  78.4 35.8 %collective-permute-start.15 = (bf16[256,768]{1,0:T(8,128)(2,1)}, bf16[256,768]{1,0:T(8,128)(2,1)S(1)}, u32[]{:S(2)}, u32[]{:S(2)}) collective-permute-start(bf16[256,768]{1,0:T(8,128)(2,1)} %get-tuple-element.35), channel_id=1, source_target_pairs={{0,4},{1,5},{2,6},{3,7},{4,0},{5,1},{6,2},{7,3},{8,12},{9,13},{10,... | collective-permute-start | bytes 1179656 | tf_op jit(solution)/shard_map/ppermute | solution.py:17
  112.5 9.2 %collective-permute-start.7 = (bf16[1,256,512]{2,1,0:T(8,128)(2,1)S(1)}, bf16[1,256,512]{2,1,0:T(8,128)(2,1)S(1)}, u32[]{:S(2)}, u32[]{:S(2)}) collective-permute-start(bf16[1,256,512]{2,1,0:T(8,128)(2,1)S(1)} %bitcast.11), channel_id=1, source_target_pairs={{0,16},{8,24},{16,0},{24,8},{1,17},{9,25},{17,1},{25,9},{2,18},{10... | collective-permute-start | bytes 786440 | tf_op jit(solution)/shard_map/ppermute | solution.py:17
  114.1 14.0 %collective-permute-start.16 = (bf16[1,256,768]{2,1,0:T(8,128)(2,1)S(1)}, bf16[1,256,768]{2,1,0:T(8,128)(2,1)S(1)}, u32[]{:S(2)}, u32[]{:S(2)}) collective-permute-start(bf16[1,256,768]{2,1,0:T(8,128)(2,1)S(1)} %bitcast.8), channel_id=1, source_target_pairs={{0,16},{8,24},{16,0},{24,8},{1,17},{9,25},{17,1},{25,9},{2,18},{10... | collective-permute-start | bytes 1179656 | tf_op jit(solution)/shard_map/ppermute | solution.py:17
  121.8 6.5 %collective-permute-start.8 = (bf16[2,256,512]{2,1,0:T(8,128)(2,1)S(1)}, bf16[2,256,512]{2,1,0:T(8,128)(2,1)S(1)}, u32[]{:S(2)}, u32[]{:S(2)}) collective-permute-start(bf16[2,256,512]{2,1,0:T(8,128)(2,1)S(1)} %pad_maximum_fusion.5), channel_id=1, source_target_pairs={{0,8},{8,0},{16,24},{24,16},{1,9},{9,1},{17,25},{25,17},{2,10},{10... | collective-permute-start | bytes 1572872 | tf_op jit(solution)/shard_map/ppermute | solution.py:17
  121.9 16.3 %collective-permute-start = (bf16[1,256,256]{2,1,0:T(8,128)(2,1)S(1)}, bf16[1,256,256]{2,1,0:T(8,128)(2,1)S(1)}, u32[]{:S(2)}, u32[]{:S(2)}) collective-permute-start(bf16[1,256,256]{2,1,0:T(8,128)(2,1)S(1)} %maximum_bitcast_fusion), channel_id=1, source_target_pairs={{0,4},{1,5},{2,6},{3,7},{4,0},{5,1},{6,2},{7,3},{8,12},{9,13},{10,... | collective-permute-start | bytes 393224 | tf_op jit(solution)/shard_map/ppermute | solution.py:17
  128.2 31.7 %collective-permute-start.17 = (bf16[2,256,768]{2,1,0:T(8,128)(2,1)S(1)}, bf16[2,256,768]{2,1,0:T(8,128)(2,1)S(1)}, u32[]{:S(2)}, u32[]{:S(2)}) collective-permute-start(bf16[2,256,768]{2,1,0:T(8,128)(2,1)S(1)} %pad_maximum_fusion.3), channel_id=1, source_target_pairs={{0,8},{8,0},{16,24},{24,16},{1,9},{9,1},{17,25},{25,17},{2,10},{10... | collective-permute-start | bytes 2359304 | tf_op jit(solution)/shard_map/ppermute | solution.py:17
  134.6 9.0 %collective-permute-start.9 = (f32[128,512]{1,0:T(8,128)}, f32[128,512]{1,0:T(8,128)S(1)}, u32[]{:S(2)}, u32[]{:S(2)}) collective-permute-start(f32[128,512]{1,0:T(8,128)} %get-tuple-element.32), channel_id=1, source_target_pairs={{0,1},{1,0},{2,3},{3,2},{4,5},{5,4},{6,7},{7,6},{8,9},{9,8},{10,11... | collective-permute-start | bytes 786440 | tf_op jit(solution)/shard_map/ppermute | solution.py:17
  136.1 9.3 %collective-permute-start.10 = (f32[128,512]{1,0:T(8,128)}, f32[128,512]{1,0:T(8,128)S(1)}, u32[]{:S(2)}, u32[]{:S(2)}) collective-permute-start(f32[128,512]{1,0:T(8,128)} %get-tuple-element.33), channel_id=1, source_target_pairs={{0,2},{1,3},{2,0},{3,1},{4,6},{5,7},{6,4},{7,5},{8,10},{9,11},{10,... | collective-permute-start | bytes 786440 | tf_op jit(solution)/shard_map/ppermute | solution.py:17
  136.1 15.1 %collective-permute-start.11 = (f32[128,512]{1,0:T(8,128)}, f32[128,512]{1,0:T(8,128)S(1)}, u32[]{:S(2)}, u32[]{:S(2)}) collective-permute-start(f32[128,512]{1,0:T(8,128)} %get-tuple-element.34), channel_id=1, source_target_pairs={{0,3},{1,2},{2,1},{3,0},{4,7},{5,6},{6,5},{7,4},{8,11},{9,10},{10,... | collective-permute-start | bytes 786440 | tf_op jit(solution)/shard_map/ppermute | solution.py:17
  138.2 18.4 %collective-permute-start.1 = (bf16[2,256,256]{2,1,0:T(8,128)(2,1)S(1)}, bf16[2,256,256]{2,1,0:T(8,128)(2,1)S(1)}, u32[]{:S(2)}, u32[]{:S(2)}) collective-permute-start(bf16[2,256,256]{2,1,0:T(8,128)(2,1)S(1)} %pad_maximum_fusion.7), channel_id=1, source_target_pairs={{0,2},{1,3},{2,0},{3,1},{4,6},{5,7},{6,4},{7,5},{8,10},{9,11},{10,... | collective-permute-start | bytes 786440 | tf_op jit(solution)/shard_map/ppermute | solution.py:17
  156.7 18.6 %collective-permute-start.2 = (bf16[4,256,256]{2,1,0:T(8,128)(2,1)S(1)}, bf16[4,256,256]{2,1,0:T(8,128)(2,1)S(1)}, u32[]{:S(2)}, u32[]{:S(2)}) collective-permute-start(bf16[4,256,256]{2,1,0:T(8,128)(2,1)S(1)} %pad_maximum_fusion.4), channel_id=1, source_target_pairs={{0,1},{1,0},{2,3},{3,2},{4,5},{5,4},{6,7},{7,6},{8,9},{9,8},{10,11... | collective-permute-start | bytes 1572872 | tf_op jit(solution)/shard_map/ppermute | solution.py:17
  163.2 14.0 %collective-permute-start.14 = (bf16[4,128,256]{2,1,0:T(8,128)(2,1)S(1)}, bf16[4,128,256]{2,1,0:T(8,128)(2,1)S(1)}, u32[]{:S(2)}, u32[]{:S(2)}) collective-permute-start(bf16[4,128,256]{2,1,0:T(8,128)(2,1)S(1)} %pad_maximum_fusion.8), channel_id=1, source_target_pairs={{0,1},{1,0},{2,3},{3,2},{4,5},{5,4},{6,7},{7,6},{8,9},{9,8},{10,11... | collective-permute-start | bytes 786440 | tf_op jit(solution)/shard_map/ppermute | solution.py:17
  171.7 20.8 %collective-permute-start.18 = (f32[128,768]{1,0:T(8,128)}, f32[128,768]{1,0:T(8,128)S(1)}, u32[]{:S(2)}, u32[]{:S(2)}) collective-permute-start(f32[128,768]{1,0:T(8,128)} %get-tuple-element.37), channel_id=1, source_target_pairs={{0,1},{1,0},{2,3},{3,2},{4,5},{5,4},{6,7},{7,6},{8,9},{9,8},{10,11... | collective-permute-start | bytes 1179656 | tf_op jit(solution)/shard_map/ppermute | solution.py:17
  171.8 20.6 %collective-permute-start.19 = (f32[128,768]{1,0:T(8,128)}, f32[128,768]{1,0:T(8,128)S(1)}, u32[]{:S(2)}, u32[]{:S(2)}) collective-permute-start(f32[128,768]{1,0:T(8,128)} %get-tuple-element.38), channel_id=1, source_target_pairs={{0,2},{1,3},{2,0},{3,1},{4,6},{5,7},{6,4},{7,5},{8,10},{9,11},{10,... | collective-permute-start | bytes 1179656 | tf_op jit(solution)/shard_map/ppermute | solution.py:17
  173.6 18.9 %collective-permute-start.20 = (f32[128,768]{1,0:T(8,128)}, f32[128,768]{1,0:T(8,128)S(1)}, u32[]{:S(2)}, u32[]{:S(2)}) collective-permute-start(f32[128,768]{1,0:T(8,128)} %get-tuple-element.39), channel_id=1, source_target_pairs={{0,3},{1,2},{2,1},{3,0},{4,7},{5,6},{6,5},{7,4},{8,11},{9,10},{10,... | collective-permute-start | bytes 1179656 | tf_op jit(solution)/shard_map/ppermute | solution.py:17
  209.7 8.9 %collective-permute-start.22 = (bf16[256,128]{1,0:T(8,128)(2,1)S(1)}, bf16[256,128]{1,0:T(8,128)(2,1)S(1)}, u32[]{:S(2)}, u32[]{:S(2)}) collective-permute-start(bf16[256,128]{1,0:T(8,128)(2,1)S(1)} %get-tuple-element.46), channel_id=1, source_target_pairs={{0,4},{1,5},{2,6},{3,7},{4,0},{5,1},{6,2},{7,3},{8,12},{9,13},{10,... | collective-permute-start | bytes 196616 | tf_op jit(solution)/shard_map/ppermute | solution.py:17
  211.8 8.9 %collective-permute-start.28 = (bf16[256,128]{1,0:T(8,128)(2,1)S(1)}, bf16[256,128]{1,0:T(8,128)(2,1)S(1)}, u32[]{:S(2)}, u32[]{:S(2)}) collective-permute-start(bf16[256,128]{1,0:T(8,128)(2,1)S(1)} %get-tuple-element.47), channel_id=1, source_target_pairs={{0,7},{1,6},{2,5},{3,4},{4,3},{5,2},{6,1},{7,0},{8,15},{9,14},{10,... | collective-permute-start | bytes 196616 | tf_op jit(solution)/shard_map/ppermute | solution.py:17
  213.2 8.1 %collective-permute-start.27 = (bf16[256,128]{1,0:T(8,128)(2,1)S(1)}, bf16[256,128]{1,0:T(8,128)(2,1)S(1)}, u32[]{:S(2)}, u32[]{:S(2)}) collective-permute-start(bf16[256,128]{1,0:T(8,128)(2,1)S(1)} %get-tuple-element.48), channel_id=1, source_target_pairs={{0,3},{1,2},{2,1},{3,0},{4,7},{5,6},{6,5},{7,4},{8,11},{9,10},{10,... | collective-permute-start | bytes 196616 | tf_op jit(solution)/shard_map/ppermute | solution.py:17
  214.1 9.3 %collective-permute-start.26 = (bf16[256,128]{1,0:T(8,128)(2,1)S(1)}, bf16[256,128]{1,0:T(8,128)(2,1)S(1)}, u32[]{:S(2)}, u32[]{:S(2)}) collective-permute-start(bf16[256,128]{1,0:T(8,128)(2,1)S(1)} %get-tuple-element.49), channel_id=1, source_target_pairs={{0,5},{1,4},{2,7},{3,6},{4,1},{5,0},{6,3},{7,2},{8,13},{9,12},{10,... | collective-permute-start | bytes 196616 | tf_op jit(solution)/shard_map/ppermute | solution.py:17
  217.0 6.4 %collective-permute-start.25 = (bf16[256,128]{1,0:T(8,128)(2,1)S(1)}, bf16[256,128]{1,0:T(8,128)(2,1)S(1)}, u32[]{:S(2)}, u32[]{:S(2)}) collective-permute-start(bf16[256,128]{1,0:T(8,128)(2,1)S(1)} %get-tuple-element.50), channel_id=1, source_target_pairs={{0,1},{1,0},{2,3},{3,2},{4,5},{5,4},{6,7},{7,6},{8,9},{9,8},{10,11... | collective-permute-start | bytes 196616 | tf_op jit(solution)/shard_map/ppermute | solution.py:17
  (18 other events, 384.2 us)

commit v2 on v1

--- a/solution.py
+++ b/solution.py
@@ -26,12 +26,18 @@
     return bits
 
 
-def doubled(block, axis, size):
-    block, order = block[None], [0]
-    for bit in bits_down(size):
-        block = jnp.concatenate([block, swap(block, axis, size, bit)])
-        order = order + [o ^ bit for o in order]
+def double(block, order, axis, size, bit):
+    return jnp.concatenate([block, swap(block, axis, size, bit)]), order + [o ^ bit for o in order]
+
+
+def finish(block, order, axis, size, bits):
+    for bit in bits:
+        block, order = double(block, order, axis, size, bit)
     return block, order
+
+
+def together(*values):
+    return lax.optimization_barrier(values)
 
 
 def params():
@@ -74,7 +80,7 @@
     out = pl.pallas_call(
         body,
         in_specs=[pl.BlockSpec(memory_space=pltpu.SMEM)] + [pl.BlockSpec(memory_space=pl.ANY)] * 4,
-        out_specs=[pl.BlockSpec(memory_space=pl.ANY)] * (inner + 1),
+        out_specs=[pl.BlockSpec(memory_space=pltpu.VMEM)] * (inner + 1),
         out_shape=[jax.ShapeDtypeStruct((tokens, 2 * rows_w), BF16)] * (inner - 1)
         + [
             jax.ShapeDtypeStruct((share, 2 * head_dim + q_cut), BF16),
@@ -88,12 +94,12 @@
     return out[: inner - 1], out[-2], out[-1]
 
 
-def multiply(where, hidden, received, near, far, order, n_fsdp):
+def multiply(where, hidden, received, near, far, order, n_fsdp, groups):
     inner = n_fsdp // 2
     tokens = hidden.shape[0]
     n_dp, share, cols = far.shape
     rows_w = n_dp * share
-    step = math.gcd(cols, 256)
+    step = 256 if all(g % 256 == 0 for g in groups) else 128
     spans = []
     at = 0
     for _, start, wide in near:
@@ -104,7 +110,7 @@
         blocks = rest[: inner - 1]
         near_refs = rest[inner - 1 : inner - 1 + len(near)]
         far_ref = rest[inner - 1 + len(near)]
-        outs = rest[inner + len(near) : 2 * inner + len(near)]
+        outs = rest[inner + len(near) : -3]
         x_all, w_all, sems = rest[-3:]
         me, dp = where_ref[0], where_ref[1]
         pairs = []
@@ -125,21 +131,26 @@
             pairs.append((far_ref.at[slot], w_all.at[pl.ds(to, share)]))
         run_copies([pltpu.make_async_copy(a, b, sems.at[i]) for i, (a, b) in enumerate(pairs)])
 
-        @pl.loop(0, cols // step)
-        def _(n):
-            at = pl.multiple_of(n * step, 128)
-            product = jnp.dot(x_all[...], w_all[:, pl.ds(at, step)], preferred_element_type=F32)
-            for k in range(inner):
-                outs[k][:, pl.ds(at, step)] = product[k * tokens : (k + 1) * tokens]
+        base = 0
+        for g, wide in enumerate(groups):
+
+            @pl.loop(0, wide // step)
+            def _(n, g=g, base=base):
+                at = pl.multiple_of(n * step, 128)
+                product = jnp.dot(x_all[...], w_all[:, pl.ds(base + at, step)], preferred_element_type=F32)
+                for k in range(inner):
+                    outs[g * inner + k][:, pl.ds(at, step)] = product[k * tokens : (k + 1) * tokens]
+
+            base += wide
 
     copies = 2 + (inner - 1) + len(near) + n_dp
     moved = inner * tokens * 2 * rows_w * 2 + 2 * rows_w * cols * 2 + inner * tokens * cols * 4
-    return pl.pallas_call(
+    out = pl.pallas_call(
         body,
         in_specs=[pl.BlockSpec(memory_space=pltpu.SMEM)]
         + [pl.BlockSpec(memory_space=pl.ANY)] * (inner + len(near) + 1),
-        out_specs=[pl.BlockSpec(memory_space=pltpu.VMEM)] * inner,
-        out_shape=[jax.ShapeDtypeStruct((tokens, cols), F32)] * inner,
+        out_specs=[pl.BlockSpec(memory_space=pltpu.VMEM)] * (inner * len(groups)),
+        out_shape=[jax.ShapeDtypeStruct((tokens, g), F32) for g in groups for _ in range(inner)],
         scratch_shapes=[
             pltpu.VMEM((inner * tokens, 2 * rows_w), BF16),
             pltpu.VMEM((2 * rows_w, cols), BF16),
@@ -151,37 +162,39 @@
         ),
         name="multiply",
     )(where, hidden, *received, *[ref for ref, _, _ in near], far)
-
-
-def attend(where, lengths, parts, q_at, d_attn, first_head, n_heads, cache, group, f_order, sums):
+    return [list(out[g * inner : (g + 1) * inner]) for g in range(len(groups))]
+
+
+def attend(where, lengths, partials, d_attn, cache, group, f_order):
     tokens = d_attn.shape[0]
     n_blocks, block, twice = cache.shape
     head_dim = twice // 2
     n_convs = lengths.shape[1]
     scale = head_dim ** (-0.5)
     to_log2 = scale * math.log2(math.e)
+    n_heads = d_attn.shape[1] // head_dim
     pair = 2 if n_heads % 2 == 0 else 1
     lanes = pair * tokens
     n_cache = n_blocks * block
     n_group = n_blocks * tokens
     chunk = 512
-    n_sum = len(sums)
-    n_part = len(parts)
+    n_part = sum(len(terms) for terms in partials)
 
     def body(where_ref, len_ref, d_ref, cache_ref, group_ref, *rest):
-        part_refs = rest[:n_part]
-        sum_refs = rest[n_part : n_part + n_sum]
-        keep_ref, give_ref, gk, gv, s_ref, p_ref, q_ref = rest[n_part + n_sum :]
+        part_refs = list(rest[:n_part])
+        keep_ref, give_ref, gk, gv, s_ref, p_ref, q_ref = rest[n_part:]
         me, dp = where_ref[0], where_ref[1]
 
-        q_all = part_refs[0][:, pl.ds(q_at, n_heads * head_dim)]
-        for ref in part_refs[1:]:
-            q_all = q_all + ref[:, pl.ds(q_at, n_heads * head_dim)]
-        q_all = q_all.astype(BF16)
-        for h in range(n_heads):
-            q_ref[h, 0] = q_all[:, h * head_dim : (h + 1) * head_dim]
-            at = (first_head + h) * head_dim
-            q_ref[h, 1] = d_ref[:, at : at + head_dim]
+        h = 0
+        for terms in partials:
+            refs, part_refs = part_refs[: len(terms)], part_refs[len(terms) :]
+            for at in range(0, terms[0].shape[1], head_dim):
+                q = refs[0][:, at : at + head_dim]
+                for ref in refs[1:]:
+                    q = q + ref[:, at : at + head_dim]
+                q_ref[h, 0] = q.astype(BF16)
+                q_ref[h, 1] = d_ref[:, h * head_dim : (h + 1) * head_dim]
+                h += 1
 
         q_pos = me * tokens + lax.broadcasted_iota(jnp.int32, (1, lanes), 1) % tokens
         begin = jnp.zeros((1, lanes), jnp.int32)
@@ -222,7 +235,6 @@
                 p = s_ref[pl.ds(n_cache + b * tokens, tokens)] * inv
                 dp_ = lax.dot_general(group_ref[b, :, head_dim:], rows_d, dims, preferred_element_type=F32)
                 delta = delta + jnp.sum(p.astype(BF16).astype(F32) * dp_, axis=0, keepdims=True)
-            first = n_sum == 0
             for b, r, size in cache_spans:
                 at = pl.ds(b * block + r, size)
                 p = s_ref[at] * inv
@@ -234,8 +246,7 @@
                 p_ref[at] = dp_
                 delta = delta + jnp.sum(pb.astype(F32) * dp_, axis=0, keepdims=True)
                 g = jnp.dot(pb, rows_d, preferred_element_type=F32)
-                before = gv[at] if first else gv[at]
-                gv[at] = jnp.where(step == 0, 0.0, before) + g
+                gv[at] = jnp.where(step == 0, 0.0, gv[at]) + g
             for b, r, size in cache_spans:
                 at = pl.ds(b * block + r, size)
                 ds = (s_ref[at] * (p_ref[at] - delta)).astype(BF16)
@@ -243,27 +254,22 @@
                 gk[at] = jnp.where(step == 0, 0.0, gk[at]) + g
 
         even = dp % 2 == 0
-        if n_sum:
-            keep_in, give_in = sum_refs[0][...], sum_refs[1][...]
-        else:
-            keep_in = give_in = 0.0
-
         @pl.when(even)
         def _():
-            keep_ref[...] = keep_in + gk[...] * scale
-            give_ref[...] = give_in + gv[...]
+            keep_ref[...] = gk[...] * scale
+            give_ref[...] = gv[...]
 
         @pl.when(jnp.logical_not(even))
         def _():
-            keep_ref[...] = keep_in + gv[...]
-            give_ref[...] = give_in + gk[...] * scale
+            keep_ref[...] = gv[...]
+            give_ref[...] = gk[...] * scale
 
     rows = n_heads * tokens
     flops = 2 * rows * head_dim * (5 * n_cache + 2 * n_group)
     return pl.pallas_call(
         body,
         in_specs=[pl.BlockSpec(memory_space=pltpu.SMEM)] * 2
-        + [pl.BlockSpec(memory_space=pltpu.VMEM)] * (3 + n_part + n_sum),
+        + [pl.BlockSpec(memory_space=pltpu.VMEM)] * (3 + n_part),
         out_specs=[pl.BlockSpec(memory_space=pltpu.VMEM)] * 2,
         out_shape=[jax.ShapeDtypeStruct((n_cache, head_dim), F32)] * 2,
         scratch_shapes=[
@@ -280,7 +286,7 @@
             transcendentals=rows * (n_cache + n_group),
         ),
         name="attend",
-    )(where, lengths, d_attn, cache, group, *parts, *sums)
+    )(where, lengths, d_attn, cache, group, *[term for terms in partials for term in terms])
 
 
 def make_on_device(n_dp, n_fsdp):
@@ -293,37 +299,51 @@
         me = lax.axis_index("fsdp")
         dp = lax.axis_index("dp")
         where = jnp.stack([me, dp]).astype(jnp.int32)
-        heads_a = heads // 4
+        heads_a = heads // 2
         q_cut = heads_a * head_dim
 
+        def from_owners(products):
+            return [products[0]] + [swap(x, "fsdp", n_fsdp, k + 1) for k, x in enumerate(products[1:])]
+
+        f_bits, d_bits = bits_down(n_fsdp), bits_down(n_dp)
+        cache = jnp.concatenate([cache_keys, cache_values], axis=1)[None]
         sent, part_a, part_b = prepare(
             where, hidden, w_query, w_key, w_value, n_dp, n_fsdp, q_cut
         )
+        cache, f_order = double(cache, [0], "fsdp", n_fsdp, f_bits[0])
         part_a = swap(part_a, "fsdp", n_fsdp, inner)
-        received = [swap(block, "fsdp", n_fsdp, k + 1) for k, block in enumerate(sent)]
+        received = [swap(block, "fsdp", n_fsdp, k + 1) for k, block in enumerate(sent[:2])]
+        part_a, cache, *received = together(part_a, cache, *received)
+        received += [swap(block, "fsdp", n_fsdp, k + 3) for k, block in enumerate(sent[2:])]
         part_b = swap(part_b, "fsdp", n_fsdp, inner)
-        cache, f_order = doubled(
-            jnp.concatenate([cache_keys, cache_values], axis=1), "fsdp", n_fsdp
-        )
-        part_a, *received = lax.optimization_barrier((part_a, *received))
-        far_a, d_order = doubled(part_a, "dp", n_dp)
-        far_b, _ = doubled(part_b, "dp", n_dp)
+        cache, f_order = double(cache, f_order, "fsdp", n_fsdp, f_bits[1])
+        far_a, d_order = double(part_a[None], [0], "dp", n_dp, d_bits[0])
+        far_a, part_b, cache, *received = together(far_a, part_b, cache, *received)
+        far_a, d_order = finish(far_a, d_order, "dp", n_dp, d_bits[1:])
+        far_b, _ = finish(part_b[None], [0], "dp", n_dp, d_bits)
+        cache, f_order = finish(cache, f_order, "fsdp", n_fsdp, f_bits[2:])
+        far_b, cache = together(far_b, cache)
 
         near_a = [(w_key, 0, head_dim), (w_value, 0, head_dim), (w_query, 0, q_cut)]
         near_b = [(w_query, q_cut, q_width - q_cut)]
-        own_a, *away_a = multiply(where, hidden, received, near_a, far_a, d_order, n_fsdp)
-        own_b, *away_b = multiply(where, hidden, received, near_b, far_b, d_order, n_fsdp)
-        parts_a = [own_a] + [swap(x, "fsdp", n_fsdp, k + 1) for k, x in enumerate(away_a)]
-        parts_b = [own_b] + [swap(x, "fsdp", n_fsdp, k + 1) for k, x in enumerate(away_b)]
-        kv_own = functools.reduce(lambda a, b: a + b, [x[:, : 2 * head_dim] for x in parts_a])
-        group, _ = doubled(kv_own.astype(BF16), "fsdp", n_fsdp)
-
-        sums = attend(
-            where, lengths, parts_a, 2 * head_dim, d_attn, 0, heads_a, cache, group, f_order, ()
+        out_kv, out_a = multiply(
+            where, hidden, received, near_a, far_a, d_order, n_fsdp, (2 * head_dim, q_cut)
         )
-        keep, give = attend(
-            where, lengths, parts_b, 0, d_attn, heads_a, heads - heads_a, cache, group, f_order, sums
+        (out_b,) = multiply(
+            where, hidden, received, near_b, far_b, d_order, n_fsdp, (q_width - q_cut,)
         )
+        parts_kv = from_owners(out_kv)
+        parts_a = from_owners(out_a)
+        *parts_kv, out_b[0] = together(*parts_kv, out_b[0])
+        parts_b = from_owners(out_b)
+        group = functools.reduce(lambda a, b: a + b, parts_kv).astype(BF16)[None]
+        group, g_order = double(group, [0], "fsdp", n_fsdp, f_bits[0])
+        group, *parts_a = together(group, *parts_a)
+        group, g_order = finish(group, g_order, "fsdp", n_fsdp, f_bits[1:-1])
+        group, *parts_b = together(group, *parts_b)
+        group, _ = finish(group, g_order, "fsdp", n_fsdp, f_bits[-1:])
+
+        keep, give = attend(where, lengths, [parts_a, parts_b], d_attn, cache, group, f_order)
 
         half = keep + swap(give, "dp", n_dp, 1)
         size = half.shape[0] // n_fsdp
@@ -331,9 +351,11 @@
         for slot in range(1, n_fsdp):
             out = half[slot * size : (slot + 1) * size].astype(BF16)
             mine = mine + swap(out, "fsdp", n_fsdp, f_order[slot]).astype(F32)
-        for bit in bits_down(n_dp)[:-1]:
+        for bit in bits_down(n_dp)[:-2]:
             mine = mine + swap(mine, "dp", n_dp, bit)
-        other = swap(mine, "dp", n_dp, 1)
+        beside, other, across = (swap(mine, "dp", n_dp, bit) for bit in (2, 1, 3))
+        mine = mine + beside
+        other = other + across
         even = dp % 2 == 0
         return jnp.where(even, mine, other), jnp.where(even, other, mine)
 

time: 233 us -> 170 us (0.73)
  Pallas kernels: 98.9 us -> 29.3 us
  starting transfers between devices: 39.3 us -> 45.3 us
  waiting for transfers between devices: 84 us -> 86.4 us
    pallas_call x1, Pallas kernels: 69.5 us -> 3.85 us  [prepare(): pl.pallas_call(body, in_specs=[pl.BlockSpec(memory_space=pltpu.SMEM)] + [...]
    ppermute x31 -> x35, starting transfers between devices: 39.3 us -> 45.3 us  [swap(): return lax.ppermute(value, axis, [(i, i ^ bit) for i in range(size)])]
    pallas_call x2 -> x1, Pallas kernels: 17.7 us -> 13.9 us  [attend(): pl.pallas_call(body, in_specs=[pl.BlockSpec(memory_space=pltpu.SMEM)] * 2...]
    ppermute x31 -> x35, waiting for transfers between devices: 84 us -> 86.4 us  [swap(): return lax.ppermute(value, axis, [(i, i ^ bit) for i in range(size)])]
  transfers between devices with their start and end apart: 31 -> 35, of which waited for: 17 -> 14; matrix products, arithmetic and copies ran while one was open for 2% -> 2% of each run, Pallas kernels for 8% -> 7%
where the time goes in v2:
time: 170 us; the launch traced here: 169 us
  waiting for transfers between devices  86.4 us (51%)
  starting transfers between devices  45.3 us (27%)
  Pallas kernels  29.3 us (17%)
  other arithmetic  7.45 us (4%)
    ppermute x35, waiting for transfers between devices, swap(): return lax.ppermute(value, axis, [(i, i ^ bit) for i in range(size)])  86.4 us
    ppermute x35, starting transfers between devices, swap(): return lax.ppermute(value, axis, [(i, i ^ bit) for i in range(size)])  45.3 us
    pallas_call x1, Pallas kernels, attend(): pl.pallas_call(body, in_specs=[pl.BlockSpec(memory_space=pltpu.SMEM)] * 2...  13.9 us
    pallas_call x2, Pallas kernels, multiply(): pl.pallas_call(body, in_specs=[pl.BlockSpec(memory_space=pltpu.SMEM)] + [...  11.5 us
    concatenate x10, other arithmetic, double(): jnp.concatenate([block, swap(block, axis, size, bit)])  4.6 us
    pallas_call x1, Pallas kernels, prepare(): pl.pallas_call(body, in_specs=[pl.BlockSpec(memory_space=pltpu.SMEM)] + [...  3.85 us
  transfers between devices with their start and end apart: 35, of which 14 were waited for; matrix products, arithmetic and copies ran while one was open for 2% of the time, Pallas kernels for 7%

profile of v2, /device:TPU:0, one launch (start us, length us, event | category | flops | bytes accessed | tf_op | source)
XLA Modules:
  0.0 169.5 jit_solution(9279904826761509464)
XLA Ops:
  1.3 3.9 %prepare.1 = (bf16[128,2048]{1,0:T(8,128)(2,1)}, bf16[128,2048]{1,0:T(8,128)(2,1)}, bf16[128,2048]{1,0:T(8,128)(2,1)}, bf16[256,768]{1,0:T(8,128)(2,1)}, bf16[256,512]{1,0:T(8,128)(2,1)}) custom-call(s32[2]{0:T(128)} %pad_add_fusion.where_ref, bf16[128,8192]{1,0:T(8,128)(2,1)} %hidden_ref.5, bf16[1024,1024]{1,0:T(8,128)(2,1)} %rest_3_.3, ...), custom_call_target="tpu_custom_call" | custom-call | bytes 4456448 | tf_op jit(solution)/shard_map/prepare/pallas_call | solution.py:80
  5.1 3.0 %collective-permute-start.2 = (bf16[128,2048]{1,0:T(8,128)(2,1)}, bf16[128,2048]{1,0:T(8,128)(2,1)S(1)}, u32[]{:S(2)}, u32[]{:S(2)}) collective-permute-start(bf16[128,2048]{1,0:T(8,128)(2,1)} %get-tuple-element.49), channel_id=1, source_target_pairs={{0,1},{1,0},{2,3},{3,2},{4,5},{5,4},{6,7},{7,6},{8,9},{9,8},{10,11... | collective-permute-start | bytes 1572872 | tf_op jit(solution)/shard_map/ppermute | solution.py:17
  9.7 2.6 %collective-permute-start = (bf16[256,768]{1,0:T(8,128)(2,1)}, bf16[256,768]{1,0:T(8,128)(2,1)S(1)}, u32[]{:S(2)}, u32[]{:S(2)}) collective-permute-start(bf16[256,768]{1,0:T(8,128)(2,1)} %get-tuple-element.48), channel_id=1, source_target_pairs={{0,4},{1,5},{2,6},{3,7},{4,0},{5,1},{6,2},{7,3},{8,12},{9,13},{10,... | collective-permute-start | bytes 1179656 | tf_op jit(solution)/shard_map/ppermute | solution.py:17
  12.8 22.5 %collective-permute-done.1 = bf16[1,256,256]{2,1,0:T(8,128)(2,1)S(1)} collective-permute-done((bf16[1,256,256]{2,1,0:T(8,128)(2,1)S(1)}, bf16[1,256,256]{2,1,0:T(8,128)(2,1)S(1)}, u32[]{:S(2)}, u32[]{:S(2)}) %collective-permute-start.1) | collective-permute-done | bytes 131104 | tf_op jit(solution)/shard_map/ppermute | solution.py:17
  40.0 19.2 %collective-permute-done.6 = bf16[2,256,256]{2,1,0:T(8,128)(2,1)S(1)} collective-permute-done((bf16[2,256,256]{2,1,0:T(8,128)(2,1)S(1)}, bf16[2,256,256]{2,1,0:T(8,128)(2,1)S(1)}, u32[]{:S(2)}, u32[]{:S(2)}) %collective-permute-start.6) | collective-permute-done | bytes 262176 | tf_op jit(solution)/shard_map/ppermute | solution.py:17
  60.6 7.8 %collective-permute-done.8 = bf16[1,256,512]{2,1,0:T(8,128)(2,1)S(1)} collective-permute-done((bf16[1,256,512]{2,1,0:T(8,128)(2,1)S(1)}, bf16[1,256,512]{2,1,0:T(8,128)(2,1)S(1)}, u32[]{:S(2)}, u32[]{:S(2)}) %collective-permute-start.8) | collective-permute-done | bytes 262176 | tf_op jit(solution)/shard_map/ppermute | solution.py:17
  68.6 5.2 %collective-permute-done.10 = bf16[4,256,256]{2,1,0:T(8,128)(2,1)S(1)} collective-permute-done((bf16[4,256,256]{2,1,0:T(8,128)(2,1)S(1)}, bf16[4,256,256]{2,1,0:T(8,128)(2,1)S(1)}, u32[]{:S(2)}, u32[]{:S(2)}) %collective-permute-start.10) | collective-permute-done | bytes 524320 | tf_op jit(solution)/shard_map/ppermute | solution.py:17
  76.2 6.3 %multiply.2 = (f32[128,256]{1,0:T(8,128)}, f32[128,256]{1,0:T(8,128)}, f32[128,256]{1,0:T(8,128)}, f32[128,256]{1,0:T(8,128)}, f32[128,512]{1,0:T(8,128)}, /*ind...) custom-call(s32[2]{0:T(128)} %pad_add_fusion.where_ref, bf16[128,8192]{1,0:T(8,128)(2,1)} %hidden_ref.5, ...), custom_call_target="tpu_custom_call" | custom-call | flops 1610612736 | bytes 6815744 | tf_op jit(solution)/shard_map/multiply/pallas_call | solution.py:148
  83.2 2.3 %collective-permute-start.13 = (f32[128,256]{1,0:T(8,128)}, f32[128,256]{1,0:T(8,128)S(1)}, u32[]{:S(2)}, u32[]{:S(2)}) collective-permute-start(f32[128,256]{1,0:T(8,128)} %get-tuple-element.66), channel_id=1, source_target_pairs={{0,2},{1,3},{2,0},{3,1},{4,6},{5,7},{6,4},{7,5},{8,10},{9,11},{10,... | collective-permute-start | bytes 393224 | tf_op jit(solution)/shard_map/ppermute | solution.py:17
  88.0 2.0 %collective-permute-start.17 = (f32[128,512]{1,0:T(8,128)S(1)}, f32[128,512]{1,0:T(8,128)S(1)}, u32[]{:S(2)}, u32[]{:S(2)}) collective-permute-start(f32[128,512]{1,0:T(8,128)S(1)} %copy-done.10), channel_id=1, source_target_pairs={{0,2},{1,3},{2,0},{3,1},{4,6},{5,7},{6,4},{7,5},{8,10},{9,11},{10,... | collective-permute-start | bytes 786440 | tf_op jit(solution)/shard_map/ppermute | solution.py:17
  90.0 5.2 %multiply.3 = (f32[128,512]{1,0:T(8,128)}, f32[128,512]{1,0:T(8,128)}, f32[128,512]{1,0:T(8,128)}, f32[128,512]{1,0:T(8,128)}) custom-call(s32[2]{0:T(128)} %pad_add_fusion.where_ref, bf16[128,8192]{1,0:T(8,128)(2,1)} %hidden_ref.5, bf16[128,2048]{1,0:T(8,128)(2,1)} %copy-done, bf16[128,2048]{1,0:T(8,128)(2,1)} %copy-done.1, bf16[128,2048]{1,0:T(8,128)(2,1)} %copy-done.2, ...), custom_call_target="tpu_custom_call" | custom-call | flops 1073741824 | bytes 5242880 | tf_op jit(solution)/shard_map/multiply/pallas_call | solution.py:148
  96.1 2.4 %collective-permute-start.15 = (bf16[1,128,256]{2,1,0:T(8,128)(2,1)S(1)}, bf16[1,128,256]{2,1,0:T(8,128)(2,1)S(1)}, u32[]{:S(2)}, u32[]{:S(2)}) collective-permute-start(bf16[1,128,256]{2,1,0:T(8,128)(2,1)S(1)} %fusion.6), channel_id=1, source_target_pairs={{0,4},{1,5},{2,6},{3,7},{4,0},{5,1},{6,2},{7,3},{8,12},{9,13},{10,... | collective-permute-start | bytes 196616 | tf_op jit(solution)/shard_map/ppermute | solution.py:17
  100.0 3.4 %collective-permute-done.15 = bf16[1,128,256]{2,1,0:T(8,128)(2,1)S(1)} collective-permute-done((bf16[1,128,256]{2,1,0:T(8,128)(2,1)S(1)}, bf16[1,128,256]{2,1,0:T(8,128)(2,1)S(1)}, u32[]{:S(2)}, u32[]{:S(2)}) %collective-permute-start.15) | collective-permute-done | bytes 65568 | tf_op jit(solution)/shard_map/ppermute | solution.py:17
  103.4 3.5 %collective-permute-start.21 = (f32[128,512]{1,0:T(8,128)}, f32[128,512]{1,0:T(8,128)S(1)}, u32[]{:S(2)}, u32[]{:S(2)}) collective-permute-start(f32[128,512]{1,0:T(8,128)} %get-tuple-element.81), channel_id=1, source_target_pairs={{0,2},{1,3},{2,0},{3,1},{4,6},{5,7},{6,4},{7,5},{8,10},{9,11},{10,... | collective-permute-start | bytes 786440 | tf_op jit(solution)/shard_map/ppermute | solution.py:17
  107.0 2.0 %collective-permute-start.19 = (bf16[2,128,256]{2,1,0:T(8,128)(2,1)S(1)}, bf16[2,128,256]{2,1,0:T(8,128)(2,1)S(1)}, u32[]{:S(2)}, u32[]{:S(2)}) collective-permute-start(bf16[2,128,256]{2,1,0:T(8,128)(2,1)S(1)} %pad_maximum_fusion.9), channel_id=1, source_target_pairs={{0,2},{1,3},{2,0},{3,1},{4,6},{5,7},{6,4},{7,5},{8,10},{9,11},{10,... | collective-permute-start | bytes 393224 | tf_op jit(solution)/shard_map/ppermute | solution.py:17
  109.0 11.4 %collective-permute-done.19 = bf16[2,128,256]{2,1,0:T(8,128)(2,1)S(1)} collective-permute-done((bf16[2,128,256]{2,1,0:T(8,128)(2,1)S(1)}, bf16[2,128,256]{2,1,0:T(8,128)(2,1)S(1)}, u32[]{:S(2)}, u32[]{:S(2)}) %collective-permute-start.19) | collective-permute-done | bytes 131104 | tf_op jit(solution)/shard_map/ppermute | solution.py:17
  121.6 5.3 %collective-permute-done.23 = bf16[4,128,256]{2,1,0:T(8,128)(2,1)S(1)} collective-permute-done((bf16[4,128,256]{2,1,0:T(8,128)(2,1)S(1)}, bf16[4,128,256]{2,1,0:T(8,128)(2,1)S(1)}, u32[]{:S(2)}, u32[]{:S(2)}) %collective-permute-start.23) | collective-permute-done | bytes 262176 | tf_op jit(solution)/shard_map/ppermute | solution.py:17
  127.8 13.9 %attend.1 = (f32[2048,128]{1,0:T(8,128)}, f32[2048,128]{1,0:T(8,128)}) custom-call(s32[2]{0:T(128)} %pad_add_fusion.where_ref, s32[1,4]{1,0:T(1,128)} %len_ref.1, bf16[128,1024]{1,0:T(8,128)(2,1)} %d_ref.1, bf16[8,256,256]{2,1,0:T(8,128)(2,1)} %pad_maximum_fusion.2.cache_ref, bf16[8,128,256]{2,1,0:T(8,128)(2,1)} %pad_maximum_fusion.6.group_ref, ...), custom_call_target="tpu_custom_call" | custom-call | flops 3221225472 | bytes 3145728 | tf_op jit(solution)/shard_map/attend/pallas_call | solution.py:269
  141.7 2.9 %collective-permute-done.24 = f32[2048,128]{1,0:T(8,128)S(1)} collective-permute-done((f32[2048,128]{1,0:T(8,128)}, f32[2048,128]{1,0:T(8,128)S(1)}, u32[]{:S(2)}, u32[]{:S(2)}) %collective-permute-start.24) | collective-permute-done | bytes 1048608 | tf_op jit(solution)/shard_map/ppermute | solution.py:17
  147.7 2.9 %collective-permute-start.31 = (bf16[256,128]{1,0:T(8,128)(2,1)S(1)}, bf16[256,128]{1,0:T(8,128)(2,1)S(1)}, u32[]{:S(2)}, u32[]{:S(2)}) collective-permute-start(bf16[256,128]{1,0:T(8,128)(2,1)S(1)} %get-tuple-element.99), channel_id=1, source_target_pairs={{0,7},{1,6},{2,5},{3,4},{4,3},{5,2},{6,1},{7,0},{8,15},{9,14},{10,... | collective-permute-start | bytes 196616 | tf_op jit(solution)/shard_map/ppermute | solution.py:17
  150.6 2.8 %collective-permute-start.29 = (bf16[256,128]{1,0:T(8,128)(2,1)S(1)}, bf16[256,128]{1,0:T(8,128)(2,1)S(1)}, u32[]{:S(2)}, u32[]{:S(2)}) collective-permute-start(bf16[256,128]{1,0:T(8,128)(2,1)S(1)} %get-tuple-element.101), channel_id=1, source_target_pairs={{0,5},{1,4},{2,7},{3,6},{4,1},{5,0},{6,3},{7,2},{8,13},{9,12},{10,... | collective-permute-start | bytes 196616 | tf_op jit(solution)/shard_map/ppermute | solution.py:17
  154.7 2.2 %collective-permute-start.27 = (bf16[256,128]{1,0:T(8,128)(2,1)S(1)}, bf16[256,128]{1,0:T(8,128)(2,1)S(1)}, u32[]{:S(2)}, u32[]{:S(2)}) collective-permute-start(bf16[256,128]{1,0:T(8,128)(2,1)S(1)} %get-tuple-element.103), channel_id=1, source_target_pairs={{0,6},{1,7},{2,4},{3,5},{4,2},{5,3},{6,0},{7,1},{8,14},{9,15},{10,... | collective-permute-start | bytes 196616 | tf_op jit(solution)/shard_map/ppermute | solution.py:17
  157.9 2.1 %collective-permute-done.29 = bf16[256,128]{1,0:T(8,128)(2,1)S(1)} collective-permute-done((bf16[256,128]{1,0:T(8,128)(2,1)S(1)}, bf16[256,128]{1,0:T(8,128)(2,1)S(1)}, u32[]{:S(2)}, u32[]{:S(2)}) %collective-permute-start.29) | collective-permute-done | bytes 65568 | tf_op jit(solution)/shard_map/ppermute | solution.py:17
  163.8 3.4 %collective-permute-done.34 = f32[256,128]{1,0:T(8,128)S(1)} collective-permute-done((f32[256,128]{1,0:T(8,128)S(1)}, f32[256,128]{1,0:T(8,128)S(1)}, u32[]{:S(2)}, u32[]{:S(2)}) %collective-permute-start.34) | collective-permute-done | bytes 131104 | tf_op jit(solution)/shard_map/ppermute | solution.py:17
  (97 shorter events, 30.3 us)
Async XLA Ops:
  5.1 30.1 %collective-permute-start.2 = (bf16[128,2048]{1,0:T(8,128)(2,1)}, bf16[128,2048]{1,0:T(8,128)(2,1)S(1)}, u32[]{:S(2)}, u32[]{:S(2)}) collective-permute-start(bf16[128,2048]{1,0:T(8,128)(2,1)} %get-tuple-element.49), channel_id=1, source_target_pairs={{0,1},{1,0},{2,3},{3,2},{4,5},{5,4},{6,7},{7,6},{8,9},{9,8},{10,11... | collective-permute-start | bytes 1572872 | tf_op jit(solution)/shard_map/ppermute | solution.py:17
  8.2 27.1 %collective-permute-start.3 = (bf16[128,2048]{1,0:T(8,128)(2,1)}, bf16[128,2048]{1,0:T(8,128)(2,1)S(1)}, u32[]{:S(2)}, u32[]{:S(2)}) collective-permute-start(bf16[128,2048]{1,0:T(8,128)(2,1)} %get-tuple-element.50), channel_id=1, source_target_pairs={{0,2},{1,3},{2,0},{3,1},{4,6},{5,7},{6,4},{7,5},{8,10},{9,11},{10,... | collective-permute-start | bytes 1572872 | tf_op jit(solution)/shard_map/ppermute | solution.py:17
  9.7 25.5 %collective-permute-start = (bf16[256,768]{1,0:T(8,128)(2,1)}, bf16[256,768]{1,0:T(8,128)(2,1)S(1)}, u32[]{:S(2)}, u32[]{:S(2)}) collective-permute-start(bf16[256,768]{1,0:T(8,128)(2,1)} %get-tuple-element.48), channel_id=1, source_target_pairs={{0,4},{1,5},{2,6},{3,7},{4,0},{5,1},{6,2},{7,3},{8,12},{9,13},{10,... | collective-permute-start | bytes 1179656 | tf_op jit(solution)/shard_map/ppermute | solution.py:17
  12.4 22.9 %collective-permute-start.1 = (bf16[1,256,256]{2,1,0:T(8,128)(2,1)S(1)}, bf16[1,256,256]{2,1,0:T(8,128)(2,1)S(1)}, u32[]{:S(2)}, u32[]{:S(2)}) collective-permute-start(bf16[1,256,256]{2,1,0:T(8,128)(2,1)S(1)} %maximum_bitcast_fusion), channel_id=1, source_target_pairs={{0,4},{1,5},{2,6},{3,7},{4,0},{5,1},{6,2},{7,3},{8,12},{9,13},{10,... | collective-permute-start | bytes 393224 | tf_op jit(solution)/shard_map/ppermute | solution.py:17
  35.3 23.9 %collective-permute-start.4 = (bf16[1,256,768]{2,1,0:T(8,128)(2,1)S(1)}, bf16[1,256,768]{2,1,0:T(8,128)(2,1)S(1)}, u32[]{:S(2)}, u32[]{:S(2)}) collective-permute-start(bf16[1,256,768]{2,1,0:T(8,128)(2,1)S(1)} %bitcast.11), channel_id=1, source_target_pairs={{0,16},{8,24},{16,0},{24,8},{1,17},{9,25},{17,1},{25,9},{2,18},{10... | collective-permute-start | bytes 1179656 | tf_op jit(solution)/shard_map/ppermute | solution.py:17
  36.9 22.4 %collective-permute-start.7 = (bf16[128,2048]{1,0:T(8,128)(2,1)}, bf16[128,2048]{1,0:T(8,128)(2,1)S(1)}, u32[]{:S(2)}, u32[]{:S(2)}) collective-permute-start(bf16[128,2048]{1,0:T(8,128)(2,1)} %get-tuple-element.56), channel_id=1, source_target_pairs={{0,3},{1,2},{2,1},{3,0},{4,7},{5,6},{6,5},{7,4},{8,11},{9,10},{10,... | collective-permute-start | bytes 1572872 | tf_op jit(solution)/shard_map/ppermute | solution.py:17
  37.3 21.9 %collective-permute-start.6 = (bf16[2,256,256]{2,1,0:T(8,128)(2,1)S(1)}, bf16[2,256,256]{2,1,0:T(8,128)(2,1)S(1)}, u32[]{:S(2)}, u32[]{:S(2)}) collective-permute-start(bf16[2,256,256]{2,1,0:T(8,128)(2,1)S(1)} %pad_maximum_fusion.7), channel_id=1, source_target_pairs={{0,2},{1,3},{2,0},{3,1},{4,6},{5,7},{6,4},{7,5},{8,10},{9,11},{10,... | collective-permute-start | bytes 786440 | tf_op jit(solution)/shard_map/ppermute | solution.py:17
  38.8 20.5 %collective-permute-start.5 = (bf16[256,512]{1,0:T(8,128)(2,1)}, bf16[256,512]{1,0:T(8,128)(2,1)S(1)}, u32[]{:S(2)}, u32[]{:S(2)}) collective-permute-start(bf16[256,512]{1,0:T(8,128)(2,1)} %get-tuple-element.52), channel_id=1, source_target_pairs={{0,4},{1,5},{2,6},{3,7},{4,0},{5,1},{6,2},{7,3},{8,12},{9,13},{10,... | collective-permute-start | bytes 786440 | tf_op jit(solution)/shard_map/ppermute | solution.py:17
  59.3 15.5 %collective-permute-start.11 = (bf16[2,256,768]{2,1,0:T(8,128)(2,1)S(1)}, bf16[2,256,768]{2,1,0:T(8,128)(2,1)S(1)}, u32[]{:S(2)}, u32[]{:S(2)}) collective-permute-start(bf16[2,256,768]{2,1,0:T(8,128)(2,1)S(1)} %pad_maximum_fusion.3), channel_id=1, source_target_pairs={{0,8},{8,0},{16,24},{24,16},{1,9},{9,1},{17,25},{25,17},{2,10},{10... | collective-permute-start | bytes 2359304 | tf_op jit(solution)/shard_map/ppermute | solution.py:17
  59.4 14.3 %collective-permute-start.10 = (bf16[4,256,256]{2,1,0:T(8,128)(2,1)S(1)}, bf16[4,256,256]{2,1,0:T(8,128)(2,1)S(1)}, u32[]{:S(2)}, u32[]{:S(2)}) collective-permute-start(bf16[4,256,256]{2,1,0:T(8,128)(2,1)S(1)} %pad_maximum_fusion.4), channel_id=1, source_target_pairs={{0,1},{1,0},{2,3},{3,2},{4,5},{5,4},{6,7},{7,6},{8,9},{9,8},{10,11... | collective-permute-start | bytes 1572872 | tf_op jit(solution)/shard_map/ppermute | solution.py:17
  68.5 17.6 %collective-permute-start.9 = (bf16[2,256,512]{2,1,0:T(8,128)(2,1)S(1)}, bf16[2,256,512]{2,1,0:T(8,128)(2,1)S(1)}, u32[]{:S(2)}, u32[]{:S(2)}) collective-permute-start(bf16[2,256,512]{2,1,0:T(8,128)(2,1)S(1)} %pad_maximum_fusion.5), channel_id=1, source_target_pairs={{0,8},{8,0},{16,24},{24,16},{1,9},{9,1},{17,25},{25,17},{2,10},{10... | collective-permute-start | bytes 1572872 | tf_op jit(solution)/shard_map/ppermute | solution.py:17
  82.5 12.7 %collective-permute-start.12 = (f32[128,256]{1,0:T(8,128)}, f32[128,256]{1,0:T(8,128)S(1)}, u32[]{:S(2)}, u32[]{:S(2)}) collective-permute-start(f32[128,256]{1,0:T(8,128)} %get-tuple-element.65), channel_id=1, source_target_pairs={{0,1},{1,0},{2,3},{3,2},{4,5},{5,4},{6,7},{7,6},{8,9},{9,8},{10,11... | collective-permute-start | bytes 393224 | tf_op jit(solution)/shard_map/ppermute | solution.py:17
  83.2 12.8 %collective-permute-start.13 = (f32[128,256]{1,0:T(8,128)}, f32[128,256]{1,0:T(8,128)S(1)}, u32[]{:S(2)}, u32[]{:S(2)}) collective-permute-start(f32[128,256]{1,0:T(8,128)} %get-tuple-element.66), channel_id=1, source_target_pairs={{0,2},{1,3},{2,0},{3,1},{4,6},{5,7},{6,4},{7,5},{8,10},{9,11},{10,... | collective-permute-start | bytes 393224 | tf_op jit(solution)/shard_map/ppermute | solution.py:17
  85.4 10.6 %collective-permute-start.14 = (f32[128,256]{1,0:T(8,128)}, f32[128,256]{1,0:T(8,128)S(1)}, u32[]{:S(2)}, u32[]{:S(2)}) collective-permute-start(f32[128,256]{1,0:T(8,128)} %get-tuple-element.67), channel_id=1, source_target_pairs={{0,3},{1,2},{2,1},{3,0},{4,7},{5,6},{6,5},{7,4},{8,11},{9,10},{10,... | collective-permute-start | bytes 393224 | tf_op jit(solution)/shard_map/ppermute | solution.py:17
  87.2 19.7 %collective-permute-start.16 = (f32[128,512]{1,0:T(8,128)S(1)}, f32[128,512]{1,0:T(8,128)S(1)}, u32[]{:S(2)}, u32[]{:S(2)}) collective-permute-start(f32[128,512]{1,0:T(8,128)S(1)} %copy-done.11), channel_id=1, source_target_pairs={{0,1},{1,0},{2,3},{3,2},{4,5},{5,4},{6,7},{7,6},{8,9},{9,8},{10,11... | collective-permute-start | bytes 786440 | tf_op jit(solution)/shard_map/ppermute | solution.py:17
  88.0 18.9 %collective-permute-start.17 = (f32[128,512]{1,0:T(8,128)S(1)}, f32[128,512]{1,0:T(8,128)S(1)}, u32[]{:S(2)}, u32[]{:S(2)}) collective-permute-start(f32[128,512]{1,0:T(8,128)S(1)} %copy-done.10), channel_id=1, source_target_pairs={{0,2},{1,3},{2,0},{3,1},{4,6},{5,7},{6,4},{7,5},{8,10},{9,11},{10,... | collective-permute-start | bytes 786440 | tf_op jit(solution)/shard_map/ppermute | solution.py:17
  95.3 11.7 %collective-permute-start.18 = (f32[128,512]{1,0:T(8,128)S(1)}, f32[128,512]{1,0:T(8,128)S(1)}, u32[]{:S(2)}, u32[]{:S(2)}) collective-permute-start(f32[128,512]{1,0:T(8,128)S(1)} %copy-done.8), channel_id=1, source_target_pairs={{0,3},{1,2},{2,1},{3,0},{4,7},{5,6},{6,5},{7,4},{8,11},{9,10},{10,... | collective-permute-start | bytes 786440 | tf_op jit(solution)/shard_map/ppermute | solution.py:17
  98.5 22.0 %collective-permute-start.20 = (f32[128,512]{1,0:T(8,128)}, f32[128,512]{1,0:T(8,128)S(1)}, u32[]{:S(2)}, u32[]{:S(2)}) collective-permute-start(f32[128,512]{1,0:T(8,128)} %get-tuple-element.80), channel_id=1, source_target_pairs={{0,1},{1,0},{2,3},{3,2},{4,5},{5,4},{6,7},{7,6},{8,9},{9,8},{10,11... | collective-permute-start | bytes 786440 | tf_op jit(solution)/shard_map/ppermute | solution.py:17
  103.4 17.0 %collective-permute-start.21 = (f32[128,512]{1,0:T(8,128)}, f32[128,512]{1,0:T(8,128)S(1)}, u32[]{:S(2)}, u32[]{:S(2)}) collective-permute-start(f32[128,512]{1,0:T(8,128)} %get-tuple-element.81), channel_id=1, source_target_pairs={{0,2},{1,3},{2,0},{3,1},{4,6},{5,7},{6,4},{7,5},{8,10},{9,11},{10,... | collective-permute-start | bytes 786440 | tf_op jit(solution)/shard_map/ppermute | solution.py:17
  106.9 13.5 %collective-permute-start.22 = (f32[128,512]{1,0:T(8,128)}, f32[128,512]{1,0:T(8,128)S(1)}, u32[]{:S(2)}, u32[]{:S(2)}) collective-permute-start(f32[128,512]{1,0:T(8,128)} %get-tuple-element.82), channel_id=1, source_target_pairs={{0,3},{1,2},{2,1},{3,0},{4,7},{5,6},{6,5},{7,4},{8,11},{9,10},{10,... | collective-permute-start | bytes 786440 | tf_op jit(solution)/shard_map/ppermute | solution.py:17
  107.0 13.4 %collective-permute-start.19 = (bf16[2,128,256]{2,1,0:T(8,128)(2,1)S(1)}, bf16[2,128,256]{2,1,0:T(8,128)(2,1)S(1)}, u32[]{:S(2)}, u32[]{:S(2)}) collective-permute-start(bf16[2,128,256]{2,1,0:T(8,128)(2,1)S(1)} %pad_maximum_fusion.9), channel_id=1, source_target_pairs={{0,2},{1,3},{2,0},{3,1},{4,6},{5,7},{6,4},{7,5},{8,10},{9,11},{10,... | collective-permute-start | bytes 393224 | tf_op jit(solution)/shard_map/ppermute | solution.py:17
  145.9 8.7 %collective-permute-start.25 = (bf16[256,128]{1,0:T(8,128)(2,1)S(1)}, bf16[256,128]{1,0:T(8,128)(2,1)S(1)}, u32[]{:S(2)}, u32[]{:S(2)}) collective-permute-start(bf16[256,128]{1,0:T(8,128)(2,1)S(1)} %get-tuple-element.98), channel_id=1, source_target_pairs={{0,4},{1,5},{2,6},{3,7},{4,0},{5,1},{6,2},{7,3},{8,12},{9,13},{10,... | collective-permute-start | bytes 196616 | tf_op jit(solution)/shard_map/ppermute | solution.py:17
  147.7 9.1 %collective-permute-start.31 = (bf16[256,128]{1,0:T(8,128)(2,1)S(1)}, bf16[256,128]{1,0:T(8,128)(2,1)S(1)}, u32[]{:S(2)}, u32[]{:S(2)}) collective-permute-start(bf16[256,128]{1,0:T(8,128)(2,1)S(1)} %get-tuple-element.99), channel_id=1, source_target_pairs={{0,7},{1,6},{2,5},{3,4},{4,3},{5,2},{6,1},{7,0},{8,15},{9,14},{10,... | collective-permute-start | bytes 196616 | tf_op jit(solution)/shard_map/ppermute | solution.py:17
  150.6 9.5 %collective-permute-start.29 = (bf16[256,128]{1,0:T(8,128)(2,1)S(1)}, bf16[256,128]{1,0:T(8,128)(2,1)S(1)}, u32[]{:S(2)}, u32[]{:S(2)}) collective-permute-start(bf16[256,128]{1,0:T(8,128)(2,1)S(1)} %get-tuple-element.101), channel_id=1, source_target_pairs={{0,5},{1,4},{2,7},{3,6},{4,1},{5,0},{6,3},{7,2},{8,13},{9,12},{10,... | collective-permute-start | bytes 196616 | tf_op jit(solution)/shard_map/ppermute | solution.py:17
  (26 other events, 281.3 us)
